TPU v7x, 32 devices: a whole 2x2x4 slice. The times are simulated.
32 devices in a mesh: adapter: 8 (over z, y), tensor: 4 (over x, core).
Axes of the slice: x: 2, y: 2, z: 4, core: 2. Of those that a mesh axis runs over, the one named last changes fastest.
Arguments:
- queries: bfloat16 [1024, 4, 4096], P('adapter', None, 'tensor'), may hold values from -160 to 160
- shared_prefix_cache: bfloat16 [2, 16, 2048, 1024], P(None, 'adapter', None, 'tensor'), may hold values from -6 to 6
- rollout_suffix_cache: bfloat16 [2, 1024, 32, 1024], P(None, 'adapter', None, 'tensor'), may hold values from -9 to 9
- fresh_key_value: bfloat16 [2, 1024, 4, 1024], P(None, 'adapter', None, 'tensor'), may hold values from -9 to 9
- rollout_prefix_index: int32 [1024], P('adapter'), may hold values from 0 to 15, as said below
- rollout_suffix_length: int32 [1024], P('adapter'), may hold values from 1 to 32, as said below
- rollout_adapter_index: int32 [1024, 1], P('adapter'), may hold values from 0 to 31; in each aligned block of 128 rows (0 to 127, 128 to 255, ...) at most 5 rows name the same one
- output_projection_weight: bfloat16 [4096, 4096], P('tensor'), may hold values from -0.75 to 0.75
- adapter_shrink_weight: bfloat16 [32, 64, 4096], P('adapter', None, 'tensor'), may hold values from -0.75 to 0.75
- adapter_expand_weight: bfloat16 [32, 64, 4096], P('adapter', None, 'tensor'), may hold values from -0.75 to 0.75
Outputs:
- mixed: bfloat16 [1024, 4, 4096], P('adapter', None, 'tensor')
Inputs may be any that keep to these rules, and one draw needn't show every extreme that they name: rollout_prefix_index[r] // 2 == r // 128: a rollout's prefix is held with it, and the rollouts of one device name each of its 2 prefixes. `rollout_suffix_length`: among the rollouts of one device some has generated 32 tokens. `rollout_adapter_index`: within the rollouts of one device (aligned blocks of 128 rows) no adapter is named more than 5 times, a bound that some block reaches.
All inputs are finite; a program needn't handle non-finite values.
Results may differ from a plain program's by a relative error of at most 0.015.
Values may be sent and summed in bfloat16 or wider, within the bound.
No kernel may reach another device: no remote copies, remote signals or barrier semaphores. Data moves between devices by JAX's collectives and lax.ppermute only.
A program may use at most 128 MiB of HBM per device.

v0:
```python
import functools
import math

import jax
import jax.numpy as jnp
from jax import lax
from jax.experimental import pallas as pl
from jax.experimental.pallas import tpu as pltpu
from jax.sharding import PartitionSpec as P

HEAD_SIZE = 128
MOST = 5
FOLD = 2
PARTS = 2
BLOCK_ROLLS = 16
KEY_CHUNK = 512
NEG = float("-inf")
MIB = 1 << 20
BRIEF = pl.CostEstimate(flops=1024, bytes_accessed=1024, transcendentals=0)
VMEM = pl.BlockSpec(memory_space=pltpu.VMEM)


def dot_nt(a, b):
    return lax.dot_general(a, b, (((1,), (1,)), ((), ())), preferred_element_type=jnp.float32)


def dot_nn(a, b):
    return jnp.dot(a, b, preferred_element_type=jnp.float32)


def attend_kernel(
    code_ref, q_ref, kv_ref, suf_ref, fr_ref, o_ref, s_ref, m_ref, *, steps, group, first, blocks
):
    prefix_count, prefix_len = kv_ref.shape[1], kv_ref.shape[2]
    key_heads = kv_ref.shape[3] // HEAD_SIZE
    rolls, suf_len = suf_ref.shape[1], suf_ref.shape[2]
    block_rows = BLOCK_ROLLS * steps
    rows = block_rows * group
    last = first + blocks - 1
    suf_rolls = HEAD_SIZE // suf_len
    suf_rows = suf_rolls * steps
    suf_groups = BLOCK_ROLLS // suf_rolls
    window_rolls = HEAD_SIZE // steps
    windows = window_rolls // BLOCK_ROLLS
    factor = HEAD_SIZE ** (-0.5) * math.log2(math.e)
    chunks = prefix_len // KEY_CHUNK
    span = prefix_len

    def row_codes(block):
        shape = (block_rows, rolls)
        mine = block * BLOCK_ROLLS + lax.broadcasted_iota(jnp.int32, shape, 0) // steps
        lane = lax.broadcasted_iota(jnp.int32, shape, 1)
        code = jnp.broadcast_to(code_ref[...].astype(jnp.float32), shape)
        col = jnp.sum(jnp.where(mine == lane, code, 0.0), axis=1, keepdims=True)
        col = jnp.broadcast_to(col, (block_rows, HEAD_SIZE)).astype(jnp.int32)
        return col // prefix_count, col % prefix_count

    def tile_rows(x):
        return jnp.concatenate([x] * group, axis=0)

    def load_q(block, h):
        start = pl.multiple_of(block * block_rows, block_rows)
        return [
            q_ref[pl.ds(start, block_rows), pl.ds((h * group + g) * HEAD_SIZE, HEAD_SIZE)]
            for g in range(group)
        ]

    def head_lanes(h):
        return pl.ds(h * HEAD_SIZE, HEAD_SIZE)

    def suffix_tile(which, block, i, h):
        start = block * BLOCK_ROLLS + i * suf_rolls
        tile = suf_ref[which, pl.ds(start, suf_rolls), :, head_lanes(h)]
        return tile.reshape(HEAD_SIZE, HEAD_SIZE)

    def fresh_tile(which, block, h):
        start = pl.multiple_of(block // windows * HEAD_SIZE, HEAD_SIZE)
        return fr_ref[which, pl.ds(start, HEAD_SIZE), head_lanes(h)]

    def prefix_tile(which, c, h):
        return jnp.concatenate(
            [
                kv_ref[which, p, pl.ds(c * KEY_CHUNK, KEY_CHUNK), head_lanes(h)]
                for p in range(prefix_count)
            ],
            axis=1,
        )

    def scores(block, h, slot):
        length, local = row_codes(block)
        parts = load_q(block, h)
        stacked = jnp.concatenate(parts, axis=0)
        wide = jnp.concatenate(
            [
                jnp.concatenate(
                    [jnp.where(local == p, x, jnp.zeros_like(x)) for x in parts], axis=0
                )
                for p in range(prefix_count)
            ],
            axis=1,
        )
        shape = (block_rows, HEAD_SIZE)
        row = lax.broadcasted_iota(jnp.int32, shape, 0)
        lane = lax.broadcasted_iota(jnp.int32, shape, 1)
        roll = row // steps
        keep = (roll % suf_rolls == lane // suf_len) & (lane % suf_len < length)
        suf_bias = jnp.where(keep, 0.0, NEG)
        in_window = (block % windows) * BLOCK_ROLLS + roll
        keep = (in_window == lane // steps) & (lane % steps <= row % steps)
        fr_bias = jnp.where(keep, 0.0, NEG)
        suf = []
        for i in range(suf_groups):
            piece = jnp.concatenate(
                [x[i * suf_rows : (i + 1) * suf_rows] for x in parts], axis=0
            )
            suf.append(dot_nt(piece, suffix_tile(0, block, i, h)))
        suf = jnp.concatenate(
            [
                jnp.concatenate([x[g * suf_rows : (g + 1) * suf_rows] for x in suf], axis=0)
                for g in range(group)
            ],
            axis=0,
        ) + tile_rows(suf_bias)
        fr = dot_nt(stacked, fresh_tile(0, block, h)) + tile_rows(fr_bias)
        s_ref[slot, :, pl.ds(span, HEAD_SIZE)] = suf
        s_ref[slot, :, pl.ds(span + HEAD_SIZE, HEAD_SIZE)] = fr
        top = jnp.maximum(suf, fr)
        yield
        for c in range(chunks):
            s = dot_nt(wide, prefix_tile(0, c, h))
            s_ref[slot, :, pl.ds(c * KEY_CHUNK, KEY_CHUNK)] = s
            for j in range(KEY_CHUNK // HEAD_SIZE):
                top = jnp.maximum(top, s[:, j * HEAD_SIZE : (j + 1) * HEAD_SIZE])
            if c == chunks - 1:
                top = jnp.max(top, axis=1, keepdims=True) * factor
                m_ref[slot] = jnp.broadcast_to(top, (rows, HEAD_SIZE))
            yield

    def outputs(block, h, slot):
        top = m_ref[slot]

        def weigh(start, width):
            x = s_ref[slot, :, pl.ds(start, width)]
            wide_top = jnp.concatenate([top] * (width // HEAD_SIZE), axis=1)
            return jnp.exp2(x * factor - wide_top)

        both = weigh(span, 2 * HEAD_SIZE)
        total = both[:, :HEAD_SIZE] + both[:, HEAD_SIZE:]
        both = both.astype(jnp.bfloat16)
        fr = dot_nn(both[:, HEAD_SIZE:], fresh_tile(1, block, h))
        suf = []
        for i in range(suf_groups):
            piece = jnp.concatenate(
                [
                    both[
                        g * block_rows + i * suf_rows : g * block_rows + (i + 1) * suf_rows,
                        :HEAD_SIZE,
                    ]
                    for g in range(group)
                ],
                axis=0,
            )
            suf.append(dot_nn(piece, suffix_tile(1, block, i, h)))
        extra = fr + jnp.concatenate(
            [
                jnp.concatenate([x[g * suf_rows : (g + 1) * suf_rows] for x in suf], axis=0)
                for g in range(group)
            ],
            axis=0,
        )
        yield
        acc = None
        for c in range(chunks):
            p = weigh(c * KEY_CHUNK, KEY_CHUNK)
            for j in range(KEY_CHUNK // HEAD_SIZE):
                total = total + p[:, j * HEAD_SIZE : (j + 1) * HEAD_SIZE]
            part = dot_nn(p.astype(jnp.bfloat16), prefix_tile(1, c, h))
            acc = part if acc is None else acc + part
            if c == chunks - 1:
                _, local = row_codes(block)
                local = tile_rows(local)
                chosen = acc[:, :HEAD_SIZE]
                for q in range(1, prefix_count):
                    chosen = jnp.where(
                        local == q, acc[:, q * HEAD_SIZE : (q + 1) * HEAD_SIZE], chosen
                    )
                weight = 1.0 / jnp.sum(total, axis=1, keepdims=True)
                out = ((chosen + extra) * weight).astype(o_ref.dtype)
                start = pl.multiple_of((block - first) * block_rows, block_rows)
                for g in range(group):
                    o_ref[
                        pl.ds(start, block_rows),
                        pl.ds((h * group + g) * HEAD_SIZE, HEAD_SIZE),
                    ] = out[g * block_rows : (g + 1) * block_rows]
            yield

    def run(*streams):
        for _ in range(chunks + 1):
            for stream in streams:
                next(stream)

    run(scores(first, 0, 0))

    def body(block, carry):
        for h in range(key_heads):
            if h + 1 < key_heads:
                run(scores(block, h + 1, h + 1), outputs(block, h, h))
            elif key_heads > 1:
                following = jnp.minimum(block + 1, last)
                run(scores(following, 0, 0), outputs(block, h, h))
            else:
                run(outputs(block, h, h))
                run(scores(jnp.minimum(block + 1, last), 0, 0))
        return carry

    lax.fori_loop(first, first + blocks, body, 0)


def attend(code, queries, prefix, suffix, fresh, steps, part):
    rows, width = queries.shape
    rows = rows // PARTS
    key_heads = prefix.shape[3] // HEAD_SIZE
    group = width // HEAD_SIZE // key_heads
    unit_rows = BLOCK_ROLLS * steps * group
    span = prefix.shape[2] + 2 * HEAD_SIZE
    blocks = suffix.shape[1] // BLOCK_ROLLS // PARTS
    return pl.pallas_call(
        functools.partial(
            attend_kernel, steps=steps, group=group, first=part * blocks, blocks=blocks
        ),
        out_shape=jax.ShapeDtypeStruct((rows, width), jnp.bfloat16),
        in_specs=[VMEM] * 5,
        out_specs=VMEM,
        scratch_shapes=[
            pltpu.VMEM((key_heads, unit_rows, span), jnp.float32),
            pltpu.VMEM((key_heads, unit_rows, HEAD_SIZE), jnp.float32),
        ],
        compiler_params=pltpu.CompilerParams(vmem_limit_bytes=30 * MIB),
        cost_estimate=BRIEF,
    )(code, queries, prefix, suffix, fresh)


def project_kernel(core_ref, a_ref, w_ref, send_ref, keep_ref, *, count):
    step = pl.program_id(0)
    part = dot_nn(a_ref[...], w_ref[...]).astype(jnp.bfloat16)

    @pl.when(step < count)
    def _():
        send_ref[0] = part

    @pl.when(step >= count)
    def _():
        keep_ref[0] = part


def project(core, attended, weight, out_width):
    rows, width = attended.shape
    count = weight.shape[1] // out_width // 2

    def column(j, core):
        parity = jnp.where(j < count, 1 - core[0], core[0])
        return (0, (j % count) * 2 + parity)

    shape = jax.ShapeDtypeStruct((count, rows, out_width), jnp.bfloat16)
    return pl.pallas_call(
        functools.partial(project_kernel, count=count),
        grid_spec=pltpu.PrefetchScalarGridSpec(
            num_scalar_prefetch=1,
            grid=(2 * count,),
            in_specs=[
                pl.BlockSpec((rows, width), lambda j, core: (0, 0)),
                pl.BlockSpec((width, out_width), column),
            ],
            out_specs=[
                pl.BlockSpec((1, rows, out_width), lambda j, core: (jnp.minimum(j, count - 1), 0, 0)),
                pl.BlockSpec((1, rows, out_width), lambda j, core: (jnp.maximum(j - count, 0), 0, 0)),
            ],
        ),
        out_shape=[shape, shape],
        compiler_params=pltpu.CompilerParams(vmem_limit_bytes=24 * MIB),
        cost_estimate=BRIEF,
    )(core, attended, weight)


def pack_kernel(target_ref, *refs):
    parts, outs = refs[:PARTS], refs[PARTS:]
    slots = outs[0].shape[0]
    part_rows = parts[0].shape[0]
    for d, out in enumerate(outs):
        total = None
        for k, part in enumerate(parts):
            row = d * slots + lax.broadcasted_iota(jnp.int32, (slots, part_rows), 0)
            chosen = row == target_ref[:, k * part_rows : (k + 1) * part_rows]
            term = dot_nn(jnp.where(chosen, 1.0, 0.0).astype(jnp.bfloat16), part[...])
            total = term if total is None else total + term
        out[...] = total.astype(jnp.bfloat16)


def pack(target, parts, count, slots):
    rows, width = parts[0].shape
    return pl.pallas_call(
        pack_kernel,
        out_shape=[jax.ShapeDtypeStruct((slots, width), jnp.bfloat16)] * count,
        in_specs=[VMEM] * (1 + len(parts)),
        out_specs=[VMEM] * count,
        compiler_params=pltpu.CompilerParams(vmem_limit_bytes=24 * MIB),
        cost_estimate=BRIEF,
    )(target, *parts)


def adapter_mask(rows, per_adapter, rank, tile):
    lane = lax.broadcasted_iota(jnp.int32, (rows, HEAD_SIZE), 1) + tile * HEAD_SIZE
    row = lax.broadcasted_iota(jnp.int32, (rows, HEAD_SIZE), 0)
    return lane // rank == row // per_adapter


def shrink_kernel(*refs, per_adapter, rank, count):
    weights, pieces, out = refs[:FOLD], refs[FOLD : FOLD + count], refs[-1]
    rows = pieces[0].shape[0] // FOLD
    for k in range(FOLD):
        span = pl.ds(k * rows, rows)
        every = dot_nt(
            jnp.concatenate([p[span, :] for p in pieces], axis=0),
            weights[k][...],
        )
        for d in range(count):
            total = None
            for tile in range(every.shape[1] // HEAD_SIZE):
                x = every[d * rows : (d + 1) * rows, tile * HEAD_SIZE : (tile + 1) * HEAD_SIZE]
                x = jnp.where(adapter_mask(rows, per_adapter, rank, tile), x, 0.0)
                total = x if total is None else total + x
            summed = total
            for turn in range(1, HEAD_SIZE // rank):
                summed = summed + pltpu.roll(total, turn * rank, axis=1)
            out[pl.ds((d * FOLD + k) * rows, rows), :] = summed


def shrink_rows(weights, pieces, per_adapter, rank):
    count = len(pieces)
    rows, width = pieces[0].shape
    return pl.pallas_call(
        functools.partial(shrink_kernel, per_adapter=per_adapter, rank=rank, count=count),
        out_shape=jax.ShapeDtypeStruct((count * rows, HEAD_SIZE), jnp.float32),
        in_specs=[VMEM] * (FOLD + count),
        out_specs=VMEM,
        compiler_params=pltpu.CompilerParams(vmem_limit_bytes=24 * MIB),
        cost_estimate=BRIEF,
    )(*weights, *pieces)


def expand_kernel(*refs, per_adapter, rank, count, terms):
    weights, sums, outs = refs[:FOLD], refs[FOLD : FOLD + terms], refs[FOLD + terms :]
    depth = weights[0].shape[0]
    rows = outs[0].shape[0] // FOLD
    for k in range(FOLD):
        spread = []
        for d in range(count):
            span = pl.ds((d * FOLD + k) * rows, rows)
            code = sums[0][span, :].astype(jnp.float32)
            for other in sums[1:]:
                code = code + other[span, :].astype(jnp.float32)
            spread.append(
                jnp.concatenate(
                    [
                        jnp.where(adapter_mask(rows, per_adapter, rank, tile), code, 0.0)
                        for tile in range(depth // HEAD_SIZE)
                    ],
                    axis=1,
                ).astype(jnp.bfloat16)
            )
        wide = dot_nn(jnp.concatenate(spread, axis=0), weights[k][...])
        wide = wide.astype(jnp.bfloat16)
        for d in range(count):
            outs[d][pl.ds(k * rows, rows), :] = wide[d * rows : (d + 1) * rows]


def expand_rows(weights, sums, per_adapter, rank, count):
    rows = sums[0].shape[0] // count
    width = weights[0].shape[1]
    return pl.pallas_call(
        functools.partial(
            expand_kernel, per_adapter=per_adapter, rank=rank, count=count, terms=len(sums)
        ),
        out_shape=[jax.ShapeDtypeStruct((rows, width), jnp.bfloat16)] * count,
        in_specs=[VMEM] * (FOLD + len(sums)),
        out_specs=[VMEM] * count,
        compiler_params=pltpu.CompilerParams(vmem_limit_bytes=24 * MIB),
        cost_estimate=BRIEF,
    )(*weights, *sums)


def combine_kernel(target_ref, *refs, count, terms):
    pieces, sums, out = refs[:count], refs[count:-1], refs[-1]
    slots = pieces[0].shape[0]
    part_rows = out.shape[0] // PARTS
    for k in range(PARTS):
        target = target_ref[pl.ds(k * part_rows, part_rows), :]
        delta = None
        for d, piece in enumerate(pieces):
            slot = d * slots + lax.broadcasted_iota(jnp.int32, (part_rows, slots), 1)
            chosen = jnp.where(target == slot, 1.0, 0.0).astype(jnp.bfloat16)
            term = dot_nn(chosen, piece[...])
            delta = term if delta is None else delta + term
        for x in sums[k * terms : (k + 1) * terms]:
            delta = delta + x[...].astype(jnp.float32)
        out[pl.ds(k * part_rows, part_rows), :] = delta.astype(jnp.bfloat16)


def combine(target, pieces, sums):
    terms = len(sums[0])
    part_rows, width = sums[0][0].shape
    count = len(pieces)
    flat = [x for part in sums for x in part]
    rows = part_rows * len(sums)
    return pl.pallas_call(
        functools.partial(combine_kernel, count=count, terms=terms),
        out_shape=jax.ShapeDtypeStruct((rows, width), jnp.bfloat16),
        in_specs=[VMEM] * (1 + count + len(flat)),
        out_specs=VMEM,
        compiler_params=pltpu.CompilerParams(vmem_limit_bytes=24 * MIB),
        cost_estimate=BRIEF,
    )(target, *pieces, *flat)


def local(
    queries,
    shared_prefix_cache,
    rollout_suffix_cache,
    fresh_key_value,
    rollout_prefix_index,
    rollout_suffix_length,
    rollout_adapter_index,
    output_projection_weight,
    adapter_shrink_weight,
    adapter_expand_weight,
):
    rolls, steps, width = queries.shape
    rows = rolls * steps
    prefix_count = shared_prefix_cache.shape[1]
    resident, rank, out_width = adapter_expand_weight.shape
    holders, sides = lax.axis_size("adapter"), lax.axis_size("tensor")
    block, chips = holders // FOLD, sides // 2
    here, side = lax.axis_index("adapter"), lax.axis_index("tensor")
    chip, core = side // 2, side % 2

    def in_block(shift):
        return [(i, i // block * block + (i + shift) % block) for i in range(holders)]

    cores = [(t, t // 2 * 2 + (t + 1) % 2) for t in range(sides)]

    def over_chips(shift):
        return [(t, (t // 2 + shift) % chips * 2 + t % 2) for t in range(sides)]

    own_shrink = adapter_shrink_weight.reshape(resident * rank, width)
    own_expand = adapter_expand_weight.reshape(resident * rank, out_width)
    shrinks, expands = [own_shrink], [own_expand]
    for fold in range(1, FOLD):
        far = [(i, (i + fold * block) % holders) for i in range(holders)]
        shrinks.append(lax.ppermute(own_shrink, "adapter", far))
        expands.append(lax.ppermute(own_expand, "adapter", far))

    adapter = rollout_adapter_index[:, 0]
    holder = adapter // resident
    order = jnp.arange(rolls, dtype=jnp.int32)
    same = (adapter[:, None] == adapter[None, :]) & (order[None, :] < order[:, None])
    turn = jnp.sum(same.astype(jnp.int32), axis=1)
    fold = (here // block - holder // block) % FOLD
    place = (holder % block - here % block) % block
    slot = ((place * FOLD + fold) * resident + adapter % resident) * MOST + turn
    target = (slot[:, None] * steps + jnp.arange(steps, dtype=jnp.int32)[None, :]).reshape(rows)
    slots = FOLD * resident * MOST * steps
    per_adapter = MOST * steps

    code = (rollout_suffix_length * prefix_count + rollout_prefix_index % prefix_count)[None, :]
    flat_queries = queries.reshape(rows, width)
    flat_fresh = fresh_key_value.reshape(2, rows, -1)
    core_index = core.reshape(1).astype(jnp.int32)
    parts, sums = [], []
    for part in range(PARTS):
        attended = attend(
            code, flat_queries, shared_prefix_cache, rollout_suffix_cache, flat_fresh, steps, part
        )
        parts.append(attended)
        send, keep = project(core_index, attended, output_projection_weight, out_width)
        pair = keep.astype(jnp.float32) + lax.ppermute(send, "tensor", cores).astype(jnp.float32)
        terms = [lax.dynamic_index_in_dim(pair, chip, 0, keepdims=False).astype(jnp.bfloat16)]
        for shift in range(1, chips):
            away = lax.dynamic_index_in_dim(pair, (chip + shift) % chips, 0, keepdims=False)
            terms.append(lax.ppermute(away.astype(jnp.bfloat16), "tensor", over_chips(shift)))
        sums.append(terms)

    parts[-1], *shrinks[1:] = lax.optimization_barrier([parts[-1]] + shrinks[1:])
    packed = pack(target[None, :], parts, block, slots)
    pieces = [packed[0]] + [
        lax.ppermute(packed[d], "adapter", in_block(d)) for d in range(1, block)
    ]
    pieces[0], *expands[1:] = lax.optimization_barrier([pieces[0]] + expands[1:])
    codes = shrink_rows(shrinks, pieces, per_adapter, rank)
    codes = codes + lax.ppermute(codes, "tensor", cores)
    brief = codes.astype(jnp.bfloat16)
    codes = [brief] + [lax.ppermute(brief, "tensor", over_chips(s)) for s in range(1, chips)]
    wide = expand_rows(expands, codes, per_adapter, rank, block)
    back = [wide[0]] + [
        lax.ppermute(wide[d], "adapter", in_block(block - d)) for d in range(1, block)
    ]
    mixed = combine(target[:, None], back, sums)
    return mixed.reshape(rolls, steps, out_width)


def solution(mesh):
    placed = (
        P("adapter", None, "tensor"),
        P(None, "adapter", None, "tensor"),
        P(None, "adapter", None, "tensor"),
        P(None, "adapter", None, "tensor"),
        P("adapter"),
        P("adapter"),
        P("adapter", None),
        P("tensor", None),
        P("adapter", None, "tensor"),
        P("adapter", None, "tensor"),
    )
    return jax.shard_map(
        local, mesh=mesh, in_specs=placed, out_specs=P("adapter", None, "tensor"), check_vma=False
    )
```

profile of v0, /device:TPU:0, one launch (start us, length us, event | category | flops | bytes accessed | tf_op | source)
XLA Modules:
  0.0 161.5 jit_solution(120845632357847193)
XLA Ops:
  0.0 1.4 reshape.70.q_ref
  1.4 0.0 copy-done.14
  1.4 0.1 reshape.71.fr_ref
  1.6 0.0 copy-done.16
  1.6 0.0 copy-done.17
  1.6 0.0 copy-start.1
  1.6 2.2 %copy-done.1 = bf16[2,2,2048,256]{3,2,1,0:T(8,128)(2,1)S(1)} copy-done((bf16[2,2,2048,256]{3,2,1,0:T(8,128)(2,1)S(1)}, bf16[2,2,2048,256]{3,2,1,0:T(8,128)(2,1)}, u32[]{:S(2)}) %copy-start.1) | copy-done | bytes 4194328
  3.8 2.2 %copy-done.3 = bf16[2,128,32,256]{3,2,1,0:T(8,128)(2,1)S(1)} copy-done((bf16[2,128,32,256]{3,2,1,0:T(8,128)(2,1)S(1)}, bf16[2,128,32,256]{3,2,1,0:T(8,128)(2,1)}, u32[]{:S(2)}) %copy-start.3) | copy-done | bytes 4194328
  6.0 9.4 %shard_map.101.refs_1_.a_ref = bf16[256,1024]{1,0:T(8,128)(2,1)S(1)} custom-call(s32[1,128]{1,0:T(1,128)S(1)} %fusion.15.code_ref, bf16[512,1024]{1,0:T(8,128)(2,1)S(1)} %reshape.70.q_ref, bf16[2,2,2048,256]{3,2,1,0:T(8,128)(2,1)S(1)} %copy-done.1, bf16[2,128,32,256]{3,2,1,0:T(8,128)(2,1)S(1)} %copy-done.3, bf16[2,512,256]{2,1,0:T(8,128)(2,1)S(1)} %reshape.71.fr_ref), custom_call_target="tpu_custom_call" | custom-call | flops 1024 | bytes 1024 | tf_op jit(solution)/shard_map/pallas_call | solution.py:227
  15.4 0.0 copy-start.2
  15.4 4.5 %shard_map.106 = (bf16[2,256,1024]{2,1,0:T(8,128)(2,1)}, bf16[2,256,1024]{2,1,0:T(8,128)(2,1)S(1)}) custom-call(s32[1]{0:T(128)} %bitcast.6.core_ref, bf16[256,1024]{1,0:T(8,128)(2,1)S(1)} %shard_map.101.refs_1_.a_ref, bf16[1024,4096]{1,0:T(8,128)(2,1)S(1)} %copy-done), custom_call_target="tpu_custom_call" | custom-call | flops 1024 | bytes 1024 | tf_op jit(solution)/shard_map/pallas_call | solution.py:265
  19.9 0.5 collective-permute-start.12
  20.4 9.4 %shard_map.100.refs_0_.a_ref = bf16[256,1024]{1,0:T(8,128)(2,1)S(1)} custom-call(s32[1,128]{1,0:T(1,128)S(1)} %fusion.15.code_ref, bf16[512,1024]{1,0:T(8,128)(2,1)S(1)} %reshape.70.q_ref, bf16[2,2,2048,256]{3,2,1,0:T(8,128)(2,1)S(1)} %copy-done.2, bf16[2,128,32,256]{3,2,1,0:T(8,128)(2,1)S(1)} %copy-done.3, bf16[2,512,256]{2,1,0:T(8,128)(2,1)S(1)} %reshape.71.fr_ref), custom_call_target="tpu_custom_call" | custom-call | flops 1024 | bytes 1024 | tf_op jit(solution)/shard_map/pallas_call | solution.py:227
  29.8 0.0 copy-start.15
  29.8 4.5 %shard_map.105 = (bf16[2,256,1024]{2,1,0:T(8,128)(2,1)}, bf16[2,256,1024]{2,1,0:T(8,128)(2,1)S(1)}) custom-call(s32[1]{0:T(128)} %bitcast.6.core_ref, bf16[256,1024]{1,0:T(8,128)(2,1)S(1)} %shard_map.100.refs_0_.a_ref, bf16[1024,4096]{1,0:T(8,128)(2,1)S(1)} %copy-done), custom_call_target="tpu_custom_call" | custom-call | flops 1024 | bytes 1024 | tf_op jit(solution)/shard_map/pallas_call | solution.py:265
  34.3 0.0 collective-permute-start.10
  34.4 4.1 %collective-permute-start = (bf16[256,1024]{1,0:T(8,128)(2,1)}, bf16[256,1024]{1,0:T(8,128)(2,1)}, u32[]{:S(2)}, u32[]{:S(2)}) collective-permute-start(bf16[256,1024]{1,0:T(8,128)(2,1)} %bitcast.5.refs_0_), channel_id=1, source_target_pairs={{0,16},{4,20},{8,24},{12,28},{16,0},{20,4},{24,8},{28,12},{1,17},{... | collective-permute-start | bytes 1572872 | tf_op jit(solution)/shard_map/ppermute | solution.py:459
  38.5 0.0 collective-permute-start.1
  38.5 0.2 convert_reduce_fusion
  38.7 0.1 iota_add_fusion
  38.8 0.1 add.128.target_ref
  38.9 35.1 %collective-permute-done.refs_1_ = bf16[256,1024]{1,0:T(8,128)(2,1)} collective-permute-done((bf16[256,1024]{1,0:T(8,128)(2,1)}, bf16[256,1024]{1,0:T(8,128)(2,1)}, u32[]{:S(2)}, u32[]{:S(2)}) %collective-permute-start) | collective-permute-done | bytes 524320 | tf_op jit(solution)/shard_map/ppermute | solution.py:459
  74.0 1.6 shard_map.102
  75.6 1.9 %collective-permute-start.2 = (bf16[160,1024]{1,0:T(8,128)(2,1)}, bf16[160,1024]{1,0:T(8,128)(2,1)S(1)}, u32[]{:S(2)}, u32[]{:S(2)}) collective-permute-start(bf16[160,1024]{1,0:T(8,128)(2,1)} %get-tuple-element.26), channel_id=1, source_target_pairs={{0,4},{4,8},{8,12},{12,0},{16,20},{20,24},{24,28},{28,16},{1,5},{5... | collective-permute-start | bytes 983048 | tf_op jit(solution)/shard_map/ppermute | solution.py:495
  77.4 0.0 collective-permute-start.3
  77.4 7.2 %collective-permute-done.1.refs_1_ = bf16[256,1024]{1,0:T(8,128)(2,1)} collective-permute-done((bf16[256,1024]{1,0:T(8,128)(2,1)}, bf16[256,1024]{1,0:T(8,128)(2,1)}, u32[]{:S(2)}, u32[]{:S(2)}) %collective-permute-start.1) | collective-permute-done | bytes 524320 | tf_op jit(solution)/shard_map/ppermute | solution.py:460
  84.7 1.6 %collective-permute-start.4 = (bf16[160,1024]{1,0:T(8,128)(2,1)}, bf16[160,1024]{1,0:T(8,128)(2,1)S(1)}, u32[]{:S(2)}, u32[]{:S(2)}) collective-permute-start(bf16[160,1024]{1,0:T(8,128)(2,1)} %get-tuple-element.28), channel_id=1, source_target_pairs={{0,12},{4,0},{8,4},{12,8},{16,28},{20,16},{24,20},{28,24},{1,13},{... | collective-permute-start | bytes 983048 | tf_op jit(solution)/shard_map/ppermute | solution.py:495
  86.3 6.3 %collective-permute-done.2.refs_3_ = bf16[160,1024]{1,0:T(8,128)(2,1)S(1)} collective-permute-done((bf16[160,1024]{1,0:T(8,128)(2,1)}, bf16[160,1024]{1,0:T(8,128)(2,1)S(1)}, u32[]{:S(2)}, u32[]{:S(2)}) %collective-permute-start.2) | collective-permute-done | bytes 327712 | tf_op jit(solution)/shard_map/ppermute | solution.py:495
  92.6 0.0 collective-permute-done.3.refs_4_
  92.6 6.9 %collective-permute-done.4.refs_5_ = bf16[160,1024]{1,0:T(8,128)(2,1)S(1)} collective-permute-done((bf16[160,1024]{1,0:T(8,128)(2,1)}, bf16[160,1024]{1,0:T(8,128)(2,1)S(1)}, u32[]{:S(2)}, u32[]{:S(2)}) %collective-permute-start.4) | collective-permute-done | bytes 327712 | tf_op jit(solution)/shard_map/ppermute | solution.py:495
  99.5 1.8 %shard_map.103 = f32[640,128]{1,0:T(8,128)S(1)} custom-call(bf16[256,1024]{1,0:T(8,128)(2,1)} %bitcast.5.refs_0_, bf16[256,1024]{1,0:T(8,128)(2,1)} %collective-permute-done.refs_1_, bf16[160,1024]{1,0:T(8,128)(2,1)S(1)} %get-tuple-element.25.refs_2_, bf16[160,1024]{1,0:T(8,128)(2,1)S(1)} %collective-permute-done.2.refs_3_, ...), custom_call_target="tpu_custom_call" | custom-call | flops 1024 | bytes 1024 | tf_op jit(solution)/shard_map/pallas_call | solution.py:341
  101.3 0.1 collective-permute-start.5
  101.4 0.0 collective-permute-done.12
  101.4 0.0 copy-done.5
  101.4 1.6 %convert_add_fusion = bf16[2,256,1024]{2,1,0:T(8,128)(2,1)S(1)} fusion(bf16[2,256,1024]{2,1,0:T(8,128)(2,1)} %collective-permute-done.12, bf16[2,256,1024]{2,1,0:T(8,128)(2,1)S(1)} %copy-done.5), kind=kLoop, calls=%fused_computation | loop fusion | flops 2097152 | bytes 3145728 | tf_op jit(solution)/shard_map/add | solution.py:485
  103.0 0.9 fusion.3
  103.9 1.5 collective-permute-start.13
  105.4 0.0 collective-permute-done.10
  105.4 1.6 %convert_add_fusion.1 = bf16[2,256,1024]{2,1,0:T(8,128)(2,1)S(1)} fusion(bf16[2,256,1024]{2,1,0:T(8,128)(2,1)} %collective-permute-done.10, bf16[2,256,1024]{2,1,0:T(8,128)(2,1)S(1)} %get-tuple-element.33), kind=kLoop, calls=%fused_computation.1 | loop fusion | flops 2097152 | bytes 3145728 | tf_op jit(solution)/shard_map/add | solution.py:485
  107.0 0.9 fusion.1
  107.9 0.5 collective-permute-start.11
  108.4 0.0 collective-permute-done.5
  108.5 1.6 collective-permute-start.6
  110.0 23.1 %collective-permute-done.6.refs_3_ = bf16[640,128]{1,0:T(8,128)(2,1)S(1)} collective-permute-done((bf16[640,128]{1,0:T(8,128)(2,1)S(1)}, bf16[640,128]{1,0:T(8,128)(2,1)S(1)}, u32[]{:S(2)}, u32[]{:S(2)}) %collective-permute-start.6) | collective-permute-done | bytes 163872 | tf_op jit(solution)/shard_map/ppermute | solution.py:501
  133.2 2.6 %shard_map.104 = (bf16[160,1024]{1,0:T(8,128)(2,1)S(1)}, bf16[160,1024]{1,0:T(8,128)(2,1)}, bf16[160,1024]{1,0:T(8,128)(2,1)}, bf16[160,1024]{1,0:T(8,128)(2,1)}) custom-call(bf16[256,1024]{1,0:T(8,128)(2,1)} %bitcast.3.refs_0_, bf16[256,1024]{1,0:T(8,128)(2,1)} %collective-permute-done.1.refs_1_, bf16[640,128]{1,0:T(8,128)(2,1)S(1)} %add_convert_fusion.refs_2_, ...), custom_call_target="tpu_custom_call" | custom-call | flops 1024 | bytes 1024 | tf_op jit(solution)/shard_map/pallas_call | solution.py:380
  135.8 0.7 copy-done.6
  136.5 0.0 collective-permute-start.7
  136.5 2.1 %collective-permute-start.8 = (bf16[160,1024]{1,0:T(8,128)(2,1)}, bf16[160,1024]{1,0:T(8,128)(2,1)S(1)}, u32[]{:S(2)}, u32[]{:S(2)}) collective-permute-start(bf16[160,1024]{1,0:T(8,128)(2,1)} %get-tuple-element.31), channel_id=1, source_target_pairs={{0,8},{4,12},{8,0},{12,4},{16,24},{20,28},{24,16},{28,20},{1,9},{5... | collective-permute-start | bytes 983048 | tf_op jit(solution)/shard_map/ppermute | solution.py:504
  138.6 0.0 collective-permute-start.9
  138.6 0.1 add.139.target_ref
  138.7 0.0 collective-permute-done.13.refs_7_
  138.7 0.0 collective-permute-done.11.refs_5_
  138.7 7.7 %collective-permute-done.7.refs_1_ = bf16[160,1024]{1,0:T(8,128)(2,1)S(1)} collective-permute-done((bf16[160,1024]{1,0:T(8,128)(2,1)}, bf16[160,1024]{1,0:T(8,128)(2,1)S(1)}, u32[]{:S(2)}, u32[]{:S(2)}) %collective-permute-start.7) | collective-permute-done | bytes 327712 | tf_op jit(solution)/shard_map/ppermute | solution.py:504
  146.5 0.7 copy-done.8
  147.2 6.0 %collective-permute-done.8.refs_2_ = bf16[160,1024]{1,0:T(8,128)(2,1)S(1)} collective-permute-done((bf16[160,1024]{1,0:T(8,128)(2,1)}, bf16[160,1024]{1,0:T(8,128)(2,1)S(1)}, u32[]{:S(2)}, u32[]{:S(2)}) %collective-permute-start.8) | collective-permute-done | bytes 327712 | tf_op jit(solution)/shard_map/ppermute | solution.py:504
  153.2 0.7 copy-done.10
  153.9 0.3 collective-permute-done.9.refs_3_
  154.3 0.7 copy-done.12
  155.0 1.0 copy-done.7
  156.0 1.0 copy-done.9
  156.9 1.0 copy-done.11
  157.9 1.0 copy-done.13
  158.9 1.4 shard_map.107
  160.3 1.2 reshape.74
  (22 shorter events, 0.1 us)
Async XLA Ops:
  0.0 1.4 copy-start.14
  0.0 1.6 copy-start.16
  0.0 1.6 copy-start.17
  1.6 2.2 %copy-start.1 = (bf16[2,2,2048,256]{3,2,1,0:T(8,128)(2,1)S(1)}, bf16[2,2,2048,256]{3,2,1,0:T(8,128)(2,1)}, u32[]{:S(2)}) copy-start(bf16[2,2,2048,256]{3,2,1,0:T(8,128)(2,1)} %kv_ref.3) | copy-start | bytes 12582916
  3.8 2.2 %copy-start.3 = (bf16[2,128,32,256]{3,2,1,0:T(8,128)(2,1)S(1)}, bf16[2,128,32,256]{3,2,1,0:T(8,128)(2,1)}, u32[]{:S(2)}) copy-start(bf16[2,128,32,256]{3,2,1,0:T(8,128)(2,1)} %suf_ref.3) | copy-start | bytes 12582916
  6.0 9.4 %copy-start = (bf16[1024,4096]{1,0:T(8,128)(2,1)S(1)}, bf16[1024,4096]{1,0:T(8,128)(2,1)}, u32[]{:S(2)}) copy-start(bf16[1024,4096]{1,0:T(8,128)(2,1)} %w_ref.3) | copy-start | bytes 25165828
  15.4 5.0 %copy-start.2 = (bf16[2,2,2048,256]{3,2,1,0:T(8,128)(2,1)S(1)}, bf16[2,2,2048,256]{3,2,1,0:T(8,128)(2,1)}, u32[]{:S(2)}) copy-start(bf16[2,2,2048,256]{3,2,1,0:T(8,128)(2,1)} %kv_ref.3) | copy-start | bytes 12582916
  19.9 9.9 %copy-start.4 = (bf16[2,256,1024]{2,1,0:T(8,128)(2,1)}, bf16[2,256,1024]{2,1,0:T(8,128)(2,1)S(1)}, u32[]{:S(2)}) copy-start(bf16[2,256,1024]{2,1,0:T(8,128)(2,1)S(1)} %get-tuple-element.35) | copy-start | bytes 3145732
  19.9 81.5 %collective-permute-start.12 = (bf16[2,256,1024]{2,1,0:T(8,128)(2,1)}, bf16[2,256,1024]{2,1,0:T(8,128)(2,1)}, u32[]{:S(2)}, u32[]{:S(2)}) collective-permute-start(bf16[2,256,1024]{2,1,0:T(8,128)(2,1)} %get-tuple-element.36), channel_id=1, source_target_pairs={{0,1},{1,0},{2,3},{3,2},{4,5},{5,4},{6,7},{7,6},{8,9},{9,8},{10,11... | collective-permute-start | bytes 3145736 | tf_op jit(solution)/shard_map/ppermute | solution.py:485
  29.8 8.7 %copy-start.15 = (s32[128,1]{0,1:T(1,128)S(1)}, s32[128,1]{0,1:T(1,128)}, u32[]{:S(2)}) copy-start(s32[128,1]{0,1:T(1,128)} %param.16) | copy-start | bytes 1540
  34.3 67.1 %copy-start.5 = (bf16[2,256,1024]{2,1,0:T(8,128)(2,1)S(1)}, bf16[2,256,1024]{2,1,0:T(8,128)(2,1)}, u32[]{:S(2)}) copy-start(bf16[2,256,1024]{2,1,0:T(8,128)(2,1)} %copy-done.4) | copy-start | bytes 3145732
  34.3 71.1 %collective-permute-start.10 = (bf16[2,256,1024]{2,1,0:T(8,128)(2,1)}, bf16[2,256,1024]{2,1,0:T(8,128)(2,1)}, u32[]{:S(2)}, u32[]{:S(2)}) collective-permute-start(bf16[2,256,1024]{2,1,0:T(8,128)(2,1)} %get-tuple-element.34), channel_id=1, source_target_pairs={{0,1},{1,0},{2,3},{3,2},{4,5},{5,4},{6,7},{7,6},{8,9},{9,8},{10,11... | collective-permute-start | bytes 3145736 | tf_op jit(solution)/shard_map/ppermute | solution.py:485
  34.4 39.6 %collective-permute-start = (bf16[256,1024]{1,0:T(8,128)(2,1)}, bf16[256,1024]{1,0:T(8,128)(2,1)}, u32[]{:S(2)}, u32[]{:S(2)}) collective-permute-start(bf16[256,1024]{1,0:T(8,128)(2,1)} %bitcast.5.refs_0_), channel_id=1, source_target_pairs={{0,16},{4,20},{8,24},{12,28},{16,0},{20,4},{24,8},{28,12},{1,17},{... | collective-permute-start | bytes 1572872 | tf_op jit(solution)/shard_map/ppermute | solution.py:459
  38.5 46.2 %collective-permute-start.1 = (bf16[256,1024]{1,0:T(8,128)(2,1)}, bf16[256,1024]{1,0:T(8,128)(2,1)}, u32[]{:S(2)}, u32[]{:S(2)}) collective-permute-start(bf16[256,1024]{1,0:T(8,128)(2,1)} %bitcast.3.refs_0_), channel_id=1, source_target_pairs={{0,16},{4,20},{8,24},{12,28},{16,0},{20,4},{24,8},{28,12},{1,17},{... | collective-permute-start | bytes 1572872 | tf_op jit(solution)/shard_map/ppermute | solution.py:460
  75.6 17.1 %collective-permute-start.2 = (bf16[160,1024]{1,0:T(8,128)(2,1)}, bf16[160,1024]{1,0:T(8,128)(2,1)S(1)}, u32[]{:S(2)}, u32[]{:S(2)}) collective-permute-start(bf16[160,1024]{1,0:T(8,128)(2,1)} %get-tuple-element.26), channel_id=1, source_target_pairs={{0,4},{4,8},{8,12},{12,0},{16,20},{20,24},{24,28},{28,16},{1,5},{5... | collective-permute-start | bytes 983048 | tf_op jit(solution)/shard_map/ppermute | solution.py:495
  77.4 15.2 %collective-permute-start.3 = (bf16[160,1024]{1,0:T(8,128)(2,1)}, bf16[160,1024]{1,0:T(8,128)(2,1)S(1)}, u32[]{:S(2)}, u32[]{:S(2)}) collective-permute-start(bf16[160,1024]{1,0:T(8,128)(2,1)} %get-tuple-element.27), channel_id=1, source_target_pairs={{0,8},{4,12},{8,0},{12,4},{16,24},{20,28},{24,16},{28,20},{1,9},{5... | collective-permute-start | bytes 983048 | tf_op jit(solution)/shard_map/ppermute | solution.py:495
  84.7 14.8 %collective-permute-start.4 = (bf16[160,1024]{1,0:T(8,128)(2,1)}, bf16[160,1024]{1,0:T(8,128)(2,1)S(1)}, u32[]{:S(2)}, u32[]{:S(2)}) collective-permute-start(bf16[160,1024]{1,0:T(8,128)(2,1)} %get-tuple-element.28), channel_id=1, source_target_pairs={{0,12},{4,0},{8,4},{12,8},{16,28},{20,16},{24,20},{28,24},{1,13},{... | collective-permute-start | bytes 983048 | tf_op jit(solution)/shard_map/ppermute | solution.py:495
  101.3 7.1 %collective-permute-start.5 = (f32[640,128]{1,0:T(8,128)S(1)}, f32[640,128]{1,0:T(8,128)S(1)}, u32[]{:S(2)}, u32[]{:S(2)}) collective-permute-start(f32[640,128]{1,0:T(8,128)S(1)} %shard_map.103), channel_id=1, source_target_pairs={{0,1},{1,0},{2,3},{3,2},{4,5},{5,4},{6,7},{7,6},{8,9},{9,8},{10,11... | collective-permute-start | bytes 983048 | tf_op jit(solution)/shard_map/ppermute | solution.py:499
  103.9 34.8 %collective-permute-start.13 = (bf16[256,1024]{1,0:T(8,128)(2,1)}, bf16[256,1024]{1,0:T(8,128)(2,1)S(1)}, u32[]{:S(2)}, u32[]{:S(2)}) collective-permute-start(bf16[256,1024]{1,0:T(8,128)(2,1)} %get-tuple-element.37), channel_id=1, source_target_pairs={{0,2},{1,3},{2,0},{3,1},{4,6},{5,7},{6,4},{7,5},{8,10},{9,11},{10,... | collective-permute-start | bytes 1572872 | tf_op jit(solution)/shard_map/ppermute | solution.py:489
  107.9 30.8 %collective-permute-start.11 = (bf16[256,1024]{1,0:T(8,128)(2,1)}, bf16[256,1024]{1,0:T(8,128)(2,1)S(1)}, u32[]{:S(2)}, u32[]{:S(2)}) collective-permute-start(bf16[256,1024]{1,0:T(8,128)(2,1)} %get-tuple-element.39), channel_id=1, source_target_pairs={{0,2},{1,3},{2,0},{3,1},{4,6},{5,7},{6,4},{7,5},{8,10},{9,11},{10,... | collective-permute-start | bytes 1572872 | tf_op jit(solution)/shard_map/ppermute | solution.py:489
  108.5 24.7 %collective-permute-start.6 = (bf16[640,128]{1,0:T(8,128)(2,1)S(1)}, bf16[640,128]{1,0:T(8,128)(2,1)S(1)}, u32[]{:S(2)}, u32[]{:S(2)}) collective-permute-start(bf16[640,128]{1,0:T(8,128)(2,1)S(1)} %add_convert_fusion.refs_2_), channel_id=1, source_target_pairs={{0,2},{1,3},{2,0},{3,1},{4,6},{5,7},{6,4},{7,5},{8,10},{9,11},{10,... | collective-permute-start | bytes 491528 | tf_op jit(solution)/shard_map/ppermute | solution.py:501
  135.8 0.7 copy-start.6
  136.5 10.0 %collective-permute-start.7 = (bf16[160,1024]{1,0:T(8,128)(2,1)}, bf16[160,1024]{1,0:T(8,128)(2,1)S(1)}, u32[]{:S(2)}, u32[]{:S(2)}) collective-permute-start(bf16[160,1024]{1,0:T(8,128)(2,1)} %get-tuple-element.30), channel_id=1, source_target_pairs={{0,12},{4,0},{8,4},{12,8},{16,28},{20,16},{24,20},{28,24},{1,13},{... | collective-permute-start | bytes 983048 | tf_op jit(solution)/shard_map/ppermute | solution.py:504
  136.5 16.6 %collective-permute-start.8 = (bf16[160,1024]{1,0:T(8,128)(2,1)}, bf16[160,1024]{1,0:T(8,128)(2,1)S(1)}, u32[]{:S(2)}, u32[]{:S(2)}) collective-permute-start(bf16[160,1024]{1,0:T(8,128)(2,1)} %get-tuple-element.31), channel_id=1, source_target_pairs={{0,8},{4,12},{8,0},{12,4},{16,24},{20,28},{24,16},{28,20},{1,9},{5... | collective-permute-start | bytes 983048 | tf_op jit(solution)/shard_map/ppermute | solution.py:504
  138.6 15.6 %collective-permute-start.9 = (bf16[160,1024]{1,0:T(8,128)(2,1)}, bf16[160,1024]{1,0:T(8,128)(2,1)S(1)}, u32[]{:S(2)}, u32[]{:S(2)}) collective-permute-start(bf16[160,1024]{1,0:T(8,128)(2,1)} %get-tuple-element.32), channel_id=1, source_target_pairs={{0,4},{4,8},{8,12},{12,0},{16,20},{20,24},{24,28},{28,16},{1,5},{5... | collective-permute-start | bytes 983048 | tf_op jit(solution)/shard_map/ppermute | solution.py:504
  146.5 0.7 copy-start.8
  153.2 0.7 copy-start.10
  154.2 0.7 copy-start.12
  155.0 1.0 copy-start.7
  156.0 1.0 copy-start.9
  156.9 1.0 copy-start.11
  157.9 1.0 copy-start.13
where the time goes:
time: 162 us; the launch traced here: 161 us
  waiting for transfers between devices  92.7 us (57%)
  Pallas kernels  35.2 us (22%)
  local copies, waits for them, and re-layouts  15.9 us (10%)
  starting transfers between devices  13.8 us (9%)
  other arithmetic  3.57 us (2%)
    ppermute x1, waiting for transfers between devices, local(): shrinks.append(lax.ppermute(own_shrink, 'adapter', far))  35.1 us
    ppermute x1, waiting for transfers between devices, local(): lax.ppermute(brief, 'tensor', over_chips(s))  23.1 us
    pallas_call x2, Pallas kernels, attend(): pl.pallas_call(functools.partial(attend_kernel, steps=steps, group=group,...  18.8 us
    ppermute x3, waiting for transfers between devices, local(): lax.ppermute(wide[d], 'adapter', in_block(block - d))  14 us
    ppermute x3, waiting for transfers between devices, local(): lax.ppermute(packed[d], 'adapter', in_block(d))  13.2 us
    unnamed x36, local copies, waits for them, and re-layouts  11.2 us
    pallas_call x2, Pallas kernels, project(): pl.pallas_call(functools.partial(project_kernel, count=count), grid_spec=...  9.08 us
    ppermute x1, waiting for transfers between devices, local(): expands.append(lax.ppermute(own_expand, 'adapter', far))  7.23 us
  transfers between devices with their start and end apart: 14, of which 8 were waited for; matrix products, arithmetic and copies ran while one was open for 3% of the time, Pallas kernels for 12%

commit v1 on v0

--- a/solution.py
+++ b/solution.py
@@ -11,12 +11,14 @@
 HEAD_SIZE = 128
 MOST = 5
 FOLD = 2
+CUTS = 2
 PARTS = 2
 BLOCK_ROLLS = 16
 KEY_CHUNK = 512
 NEG = float("-inf")
 MIB = 1 << 20
 BRIEF = pl.CostEstimate(flops=1024, bytes_accessed=1024, transcendentals=0)
+LENGTHY = pl.CostEstimate(flops=1 << 33, bytes_accessed=1 << 24, transcendentals=0)
 VMEM = pl.BlockSpec(memory_space=pltpu.VMEM)
 
 
@@ -235,8 +237,8 @@
             pltpu.VMEM((key_heads, unit_rows, span), jnp.float32),
             pltpu.VMEM((key_heads, unit_rows, HEAD_SIZE), jnp.float32),
         ],
-        compiler_params=pltpu.CompilerParams(vmem_limit_bytes=30 * MIB),
-        cost_estimate=BRIEF,
+        compiler_params=pltpu.CompilerParams(vmem_limit_bytes=20 * MIB),
+        cost_estimate=LENGTHY,
     )(code, queries, prefix, suffix, fresh)
 
 
@@ -277,9 +279,29 @@
             ],
         ),
         out_shape=[shape, shape],
-        compiler_params=pltpu.CompilerParams(vmem_limit_bytes=24 * MIB),
+        compiler_params=pltpu.CompilerParams(vmem_limit_bytes=8 * MIB),
         cost_estimate=BRIEF,
     )(core, attended, weight)
+
+
+def pair_kernel(chip_ref, keep_ref, come_ref, *outs):
+    chips = len(outs)
+    for shift, out in enumerate(outs):
+        index = (chip_ref[0] + shift) % chips
+        pair = keep_ref[index].astype(jnp.float32) + come_ref[index].astype(jnp.float32)
+        out[...] = pair.astype(jnp.bfloat16)
+
+
+def pair_sums(chip, keep, come):
+    chips, rows, width = keep.shape
+    return pl.pallas_call(
+        pair_kernel,
+        out_shape=[jax.ShapeDtypeStruct((rows, width), jnp.bfloat16)] * chips,
+        in_specs=[pl.BlockSpec(memory_space=pltpu.SMEM), VMEM, VMEM],
+        out_specs=[VMEM] * chips,
+        compiler_params=pltpu.CompilerParams(vmem_limit_bytes=8 * MIB),
+        cost_estimate=BRIEF,
+    )(chip, keep, come)
 
 
 def pack_kernel(target_ref, *refs):
@@ -303,7 +325,7 @@
         out_shape=[jax.ShapeDtypeStruct((slots, width), jnp.bfloat16)] * count,
         in_specs=[VMEM] * (1 + len(parts)),
         out_specs=[VMEM] * count,
-        compiler_params=pltpu.CompilerParams(vmem_limit_bytes=24 * MIB),
+        compiler_params=pltpu.CompilerParams(vmem_limit_bytes=8 * MIB),
         cost_estimate=BRIEF,
     )(target, *parts)
 
@@ -343,14 +365,15 @@
         out_shape=jax.ShapeDtypeStruct((count * rows, HEAD_SIZE), jnp.float32),
         in_specs=[VMEM] * (FOLD + count),
         out_specs=VMEM,
-        compiler_params=pltpu.CompilerParams(vmem_limit_bytes=24 * MIB),
-        cost_estimate=BRIEF,
+        compiler_params=pltpu.CompilerParams(vmem_limit_bytes=8 * MIB),
+        cost_estimate=LENGTHY,
     )(*weights, *pieces)
 
 
 def expand_kernel(*refs, per_adapter, rank, count, terms):
-    weights, sums, outs = refs[:FOLD], refs[FOLD : FOLD + terms], refs[FOLD + terms :]
-    depth = weights[0].shape[0]
+    own, sums, outs = refs[0], refs[1 + CUTS : 1 + CUTS + terms], refs[1 + CUTS + terms :]
+    weights = [own[...], jnp.concatenate([x[...] for x in refs[1 : 1 + CUTS]], axis=0)]
+    depth = own.shape[0]
     rows = outs[0].shape[0] // FOLD
     for k in range(FOLD):
         spread = []
@@ -368,7 +391,7 @@
                     axis=1,
                 ).astype(jnp.bfloat16)
             )
-        wide = dot_nn(jnp.concatenate(spread, axis=0), weights[k][...])
+        wide = dot_nn(jnp.concatenate(spread, axis=0), weights[k])
         wide = wide.astype(jnp.bfloat16)
         for d in range(count):
             outs[d][pl.ds(k * rows, rows), :] = wide[d * rows : (d + 1) * rows]
@@ -382,9 +405,9 @@
             expand_kernel, per_adapter=per_adapter, rank=rank, count=count, terms=len(sums)
         ),
         out_shape=[jax.ShapeDtypeStruct((rows, width), jnp.bfloat16)] * count,
-        in_specs=[VMEM] * (FOLD + len(sums)),
+        in_specs=[VMEM] * (1 + CUTS + len(sums)),
         out_specs=[VMEM] * count,
-        compiler_params=pltpu.CompilerParams(vmem_limit_bytes=24 * MIB),
+        compiler_params=pltpu.CompilerParams(vmem_limit_bytes=8 * MIB),
         cost_estimate=BRIEF,
     )(*weights, *sums)
 
@@ -417,7 +440,7 @@
         out_shape=jax.ShapeDtypeStruct((rows, width), jnp.bfloat16),
         in_specs=[VMEM] * (1 + count + len(flat)),
         out_specs=VMEM,
-        compiler_params=pltpu.CompilerParams(vmem_limit_bytes=24 * MIB),
+        compiler_params=pltpu.CompilerParams(vmem_limit_bytes=8 * MIB),
         cost_estimate=BRIEF,
     )(target, *pieces, *flat)
 
@@ -453,11 +476,7 @@
 
     own_shrink = adapter_shrink_weight.reshape(resident * rank, width)
     own_expand = adapter_expand_weight.reshape(resident * rank, out_width)
-    shrinks, expands = [own_shrink], [own_expand]
-    for fold in range(1, FOLD):
-        far = [(i, (i + fold * block) % holders) for i in range(holders)]
-        shrinks.append(lax.ppermute(own_shrink, "adapter", far))
-        expands.append(lax.ppermute(own_expand, "adapter", far))
+    far = [(i, (i + block) % holders) for i in range(holders)]
 
     adapter = rollout_adapter_index[:, 0]
     holder = adapter // resident
@@ -475,34 +494,50 @@
     flat_queries = queries.reshape(rows, width)
     flat_fresh = fresh_key_value.reshape(2, rows, -1)
     core_index = core.reshape(1).astype(jnp.int32)
-    parts, sums = [], []
-    for part in range(PARTS):
-        attended = attend(
+    chip_index = chip.reshape(1).astype(jnp.int32)
+    cut = own_expand.shape[0] // CUTS
+    cuts = [own_expand[k * cut : (k + 1) * cut] for k in range(CUTS)]
+    tie = lax.optimization_barrier
+
+    def attend_part(code, part):
+        return attend(
             code, flat_queries, shared_prefix_cache, rollout_suffix_cache, flat_fresh, steps, part
         )
-        parts.append(attended)
-        send, keep = project(core_index, attended, output_projection_weight, out_width)
-        pair = keep.astype(jnp.float32) + lax.ppermute(send, "tensor", cores).astype(jnp.float32)
-        terms = [lax.dynamic_index_in_dim(pair, chip, 0, keepdims=False).astype(jnp.bfloat16)]
-        for shift in range(1, chips):
-            away = lax.dynamic_index_in_dim(pair, (chip + shift) % chips, 0, keepdims=False)
-            terms.append(lax.ppermute(away.astype(jnp.bfloat16), "tensor", over_chips(shift)))
-        sums.append(terms)
-
-    parts[-1], *shrinks[1:] = lax.optimization_barrier([parts[-1]] + shrinks[1:])
-    packed = pack(target[None, :], parts, block, slots)
+
+    def send_over_chips(pairs):
+        return [lax.ppermute(pairs[s], "tensor", over_chips(s)) for s in range(1, chips)]
+
+    code, target, cuts = tie((code, target, cuts))
+    shrink = lax.ppermute(own_shrink, "adapter", far)
+    first = attend_part(code, 0)
+    send, keep = project(core_index, first, output_projection_weight, out_width)
+    come = lax.ppermute(send, "tensor", cores)
+    code, shrink, keep, cuts[0] = tie((code, shrink, keep, cuts[0]))
+    expands = [lax.ppermute(cuts[0], "adapter", far)]
+    second = attend_part(code, 1)
+    pairs = pair_sums(chip_index, keep, come)
+    second, expands[0], cuts[1], *pairs = tie((second, expands[0], cuts[1], *pairs))
+    expands.append(lax.ppermute(cuts[1], "adapter", far))
+    early = send_over_chips(pairs)
+    packed = list(pack(target[None, :], [first, second], block, slots))
+    second, packed[0] = tie((second, packed[0]))
     pieces = [packed[0]] + [
         lax.ppermute(packed[d], "adapter", in_block(d)) for d in range(1, block)
     ]
-    pieces[0], *expands[1:] = lax.optimization_barrier([pieces[0]] + expands[1:])
-    codes = shrink_rows(shrinks, pieces, per_adapter, rank)
+    send, keep = project(core_index, second, output_projection_weight, out_width)
+    late_pairs = pair_sums(chip_index, keep, lax.ppermute(send, "tensor", cores))
+    pieces[0], expands[1], early = tie((pieces[0], expands[1], early))
+    codes = shrink_rows([own_shrink, shrink], pieces, per_adapter, rank)
     codes = codes + lax.ppermute(codes, "tensor", cores)
     brief = codes.astype(jnp.bfloat16)
     codes = [brief] + [lax.ppermute(brief, "tensor", over_chips(s)) for s in range(1, chips)]
-    wide = expand_rows(expands, codes, per_adapter, rank, block)
+    codes, late_pairs = tie((codes, late_pairs))
+    late = send_over_chips(late_pairs)
+    wide = expand_rows([own_expand, *expands], codes, per_adapter, rank, block)
     back = [wide[0]] + [
         lax.ppermute(wide[d], "adapter", in_block(block - d)) for d in range(1, block)
     ]
+    sums = [[pairs[0], *early], [late_pairs[0], *late]]
     mixed = combine(target[:, None], back, sums)
     return mixed.reshape(rolls, steps, out_width)
 

time: 162 us -> 112 us (0.69)
  waiting for transfers between devices: 92.7 us -> 31.5 us
  local copies, waits for them, and re-layouts: 15.9 us -> 23.5 us
  starting transfers between devices: 13.8 us -> 18.8 us
    ppermute x6 -> x7, waiting for transfers between devices: 42.3 us -> 12.5 us  [the longest x1 12.5 us: local(): expands.append(lax.ppermute(cuts[1], 'adapter', far))]
    ppermute x1, waiting for transfers between devices: 23.1 us -> 4.96 us  [local(): lax.ppermute(brief, 'tensor', over_chips(s))]
    ppermute x3, waiting for transfers between devices: 13.2 us -> 0.01 us  [local(): lax.ppermute(packed[d], 'adapter', in_block(d))]
    unnamed x36 -> x32, local copies, waits for them, and re-layouts: 11.2 us -> 17.7 us
    add x2 -> x0, other arithmetic: 3.23 us -> none  [local(): keep.astype(jnp.float32)]
    ppermute x3, starting transfers between devices: 2.08 us -> 4.82 us  [local(): lax.ppermute(wide[d], 'adapter', in_block(block - d))]
    slice x0 -> x1, local copies, waits for them, and re-layouts: none -> 1.79 us  [local(): cuts = [own_expand[k * cut:(k + 1) * cut] for k in range(CUTS)]]
    convert_element_type x2 -> x0, local copies, waits for them, and re-layouts: 1.73 us -> none  [local(): away.astype(jnp.bfloat16)]
  transfers between devices with their start and end apart: 14 -> 15, of which waited for: 8 -> 6; matrix products, arithmetic and copies ran while one was open for 3% -> 6% of each run, Pallas kernels for 12% -> 29%
where the time goes in v1:
time: 112 us; the launch traced here: 111 us
  Pallas kernels  34.7 us (31%)
  waiting for transfers between devices  31.5 us (28%)
  local copies, waits for them, and re-layouts  23.5 us (21%)
  starting transfers between devices  18.8 us (17%)
  other arithmetic  2.38 us (2%)
    pallas_call x2, Pallas kernels, attend(): pl.pallas_call(functools.partial(attend_kernel, steps=steps, group=group,...  18.8 us
    unnamed x32, local copies, waits for them, and re-layouts  17.7 us
    ppermute x3, waiting for transfers between devices, local(): lax.ppermute(wide[d], 'adapter', in_block(block - d))  12.8 us
    ppermute x1, waiting for transfers between devices, local(): expands.append(lax.ppermute(cuts[1], 'adapter', far))  12.5 us
    pallas_call x2, Pallas kernels, project(): pl.pallas_call(functools.partial(project_kernel, count=count), grid_spec=...  8.23 us
    ppermute x1, waiting for transfers between devices, local(): lax.ppermute(brief, 'tensor', over_chips(s))  4.96 us
    ppermute x3, starting transfers between devices, local(): lax.ppermute(wide[d], 'adapter', in_block(block - d))  4.82 us
    ppermute x3, starting transfers between devices, local(): lax.ppermute(packed[d], 'adapter', in_block(d))  4.55 us
  transfers between devices with their start and end apart: 15, of which 6 were waited for; matrix products, arithmetic and copies ran while one was open for 6% of the time, Pallas kernels for 29%

profile of v1, /device:TPU:0, one launch (start us, length us, event | category | flops | bytes accessed | tf_op | source)
XLA Modules:
  0.0 111.0 jit_solution(17275815881933747304)
XLA Ops:
  0.0 4.0 %collective-permute-start = (bf16[256,1024]{1,0:T(8,128)(2,1)}, bf16[256,1024]{1,0:T(8,128)(2,1)}, u32[]{:S(2)}, u32[]{:S(2)}) collective-permute-start(bf16[256,1024]{1,0:T(8,128)(2,1)} %bitcast.24), channel_id=1, source_target_pairs={{0,16},{4,20},{8,24},{12,28},{16,0},{20,4},{24,8},{28,12},{1,17},{... | collective-permute-start | bytes 1572872 | tf_op jit(solution)/shard_map/ppermute | solution.py:511
  4.0 0.9 convert_reduce_fusion
  5.0 0.7 fusion.10
  5.6 0.1 iota_add_fusion
  5.7 0.1 add.90
  5.8 1.2 %reshape.34.fr_ref = bf16[2,512,256]{2,1,0:T(8,128)(2,1)S(1)} reshape(bf16[2,128,4,256]{3,2,1,0:T(4,128)(2,1)} %param.13) | data formatting | bytes 1048576 | tf_op jit(solution)/shard_map/reshape | solution.py:495
  7.0 1.8 %fusion.12 = (bf16[2,64,1024]{2,1,0:T(8,128)(2,1)}, bf16[2,64,1024]{2,1,0:T(8,128)(2,1)S(1)}) fusion(bf16[4,64,1024]{2,1,0:T(8,128)(2,1)} %param.19), kind=kLoop, calls=%fused_computation.36 | loop fusion | bytes 1048576 | tf_op jit(solution)/shard_map/slice | solution.py:499
  8.8 0.7 fusion.11.code_ref
  9.5 1.3 %reshape.33.q_ref = bf16[512,1024]{1,0:T(8,128)(2,1)S(1)} reshape(bf16[128,4,1024]{2,1,0:T(4,128)(2,1)} %param.10) | data formatting | bytes 2097152 | tf_op jit(solution)/shard_map/reshape | solution.py:494
  10.8 0.0 copy-start.8
  10.8 2.2 %copy-done.8 = bf16[2,2,2048,256]{3,2,1,0:T(8,128)(2,1)S(1)} copy-done((bf16[2,2,2048,256]{3,2,1,0:T(8,128)(2,1)S(1)}, bf16[2,2,2048,256]{3,2,1,0:T(8,128)(2,1)}, u32[]{:S(2)}) %copy-start.8) | copy-done | bytes 4194328
  13.0 2.2 %copy-done.10 = bf16[2,128,32,256]{3,2,1,0:T(8,128)(2,1)S(1)} copy-done((bf16[2,128,32,256]{3,2,1,0:T(8,128)(2,1)S(1)}, bf16[2,128,32,256]{3,2,1,0:T(8,128)(2,1)}, u32[]{:S(2)}) %copy-start.10) | copy-done | bytes 4194328
  15.2 9.4 %shard_map.100.a_ref.refs_0_ = bf16[256,1024]{1,0:T(8,128)(2,1)S(1)} custom-call(s32[1,128]{1,0:T(1,128)S(1)} %fusion.11.code_ref, bf16[512,1024]{1,0:T(8,128)(2,1)S(1)} %reshape.33.q_ref, bf16[2,2,2048,256]{3,2,1,0:T(8,128)(2,1)S(1)} %copy-done.8, bf16[2,128,32,256]{3,2,1,0:T(8,128)(2,1)S(1)} %copy-done.10, bf16[2,512,256]{2,1,0:T(8,128)(2,1)S(1)} %reshape.34.fr_ref), custom_call_target="tpu_custom_call" | custom-call | flops 8589934592 | bytes 16777216 | tf_op jit(solution)/shard_map/pallas_call | solution.py:229
  24.6 0.0 copy-start
  24.6 3.4 %copy-done = bf16[1024,4096]{1,0:T(8,128)(2,1)S(1)} copy-done((bf16[1024,4096]{1,0:T(8,128)(2,1)S(1)}, bf16[1024,4096]{1,0:T(8,128)(2,1)}, u32[]{:S(2)}) %copy-start) | copy-done | bytes 8388632
  28.0 4.5 %shard_map.101 = (bf16[2,256,1024]{2,1,0:T(8,128)(2,1)}, bf16[2,256,1024]{2,1,0:T(8,128)(2,1)S(1)}) custom-call(s32[1]{0:T(128)} %bitcast.9.core_ref, bf16[256,1024]{1,0:T(8,128)(2,1)S(1)} %shard_map.100.a_ref.refs_0_, bf16[1024,4096]{1,0:T(8,128)(2,1)S(1)} %copy-done), custom_call_target="tpu_custom_call" | custom-call | flops 1024 | bytes 1024 | tf_op jit(solution)/shard_map/pallas_call | solution.py:267
  32.5 0.0 collective-permute-start.2
  32.5 0.0 collective-permute-done.refs_1_
  32.5 0.0 slice-start.1
  32.5 0.1 collective-permute-start.1
  32.6 0.0 copy-start.3
  32.6 1.4 %copy-done.3 = bf16[512,1024]{1,0:T(8,128)(2,1)S(1)} copy-done((bf16[512,1024]{1,0:T(8,128)(2,1)S(1)}, bf16[512,1024]{1,0:T(8,128)(2,1)}, u32[]{:S(2)}) %copy-start.3) | copy-done | bytes 1048600
  34.0 2.9 %copy-done.9 = bf16[2,2,2048,256]{3,2,1,0:T(8,128)(2,1)S(1)} copy-done((bf16[2,2,2048,256]{3,2,1,0:T(8,128)(2,1)S(1)}, bf16[2,2,2048,256]{3,2,1,0:T(8,128)(2,1)}, u32[]{:S(2)}) %copy-start.9) | copy-done | bytes 4194328
  36.9 2.2 %copy-done.11 = bf16[2,128,32,256]{3,2,1,0:T(8,128)(2,1)S(1)} copy-done((bf16[2,128,32,256]{3,2,1,0:T(8,128)(2,1)S(1)}, bf16[2,128,32,256]{3,2,1,0:T(8,128)(2,1)}, u32[]{:S(2)}) %copy-start.11) | copy-done | bytes 4194328
  39.1 9.4 %shard_map.102.refs_1_.a_ref = bf16[256,1024]{1,0:T(8,128)(2,1)S(1)} custom-call(s32[1,128]{1,0:T(1,128)S(1)} %fusion.11.code_ref, bf16[512,1024]{1,0:T(8,128)(2,1)S(1)} %copy-done.3, bf16[2,2,2048,256]{3,2,1,0:T(8,128)(2,1)S(1)} %copy-done.9, bf16[2,128,32,256]{3,2,1,0:T(8,128)(2,1)S(1)} %copy-done.11, bf16[2,512,256]{2,1,0:T(8,128)(2,1)S(1)} %reshape.34.fr_ref), custom_call_target="tpu_custom_call" | custom-call | flops 8589934592 | bytes 16777216 | tf_op jit(solution)/shard_map/pallas_call | solution.py:229
  48.5 0.0 collective-permute-done.2.come_ref
  48.5 0.2 shard_map.103
  48.7 0.0 collective-permute-done.1.refs_1_
  48.7 2.0 %collective-permute-start.4 = (bf16[256,1024]{1,0:T(8,128)(2,1)S(1)}, bf16[256,1024]{1,0:T(8,128)(2,1)S(1)}, u32[]{:S(2)}, u32[]{:S(2)}) collective-permute-start(bf16[256,1024]{1,0:T(8,128)(2,1)S(1)} %get-tuple-element.59), channel_id=1, source_target_pairs={{0,2},{1,3},{2,0},{3,1},{4,6},{5,7},{6,4},{7,5},{8,10},{9,11},{10,... | collective-permute-start | bytes 1572872 | tf_op jit(solution)/shard_map/ppermute | solution.py:508
  50.7 0.9 shard_map.104
  51.6 1.6 %collective-permute-start.5 = (bf16[160,1024]{1,0:T(8,128)(2,1)S(1)}, bf16[160,1024]{1,0:T(8,128)(2,1)S(1)}, u32[]{:S(2)}, u32[]{:S(2)}) collective-permute-start(bf16[160,1024]{1,0:T(8,128)(2,1)S(1)} %get-tuple-element.63), channel_id=1, source_target_pairs={{0,4},{4,8},{8,12},{12,0},{16,20},{20,24},{24,28},{28,16},{1,5},{5... | collective-permute-start | bytes 983048 | tf_op jit(solution)/shard_map/ppermute | solution.py:525
  53.2 1.5 %collective-permute-start.6 = (bf16[160,1024]{1,0:T(8,128)(2,1)S(1)}, bf16[160,1024]{1,0:T(8,128)(2,1)S(1)}, u32[]{:S(2)}, u32[]{:S(2)}) collective-permute-start(bf16[160,1024]{1,0:T(8,128)(2,1)S(1)} %get-tuple-element.64), channel_id=1, source_target_pairs={{0,8},{4,12},{8,0},{12,4},{16,24},{20,28},{24,16},{28,20},{1,9},{5... | collective-permute-start | bytes 983048 | tf_op jit(solution)/shard_map/ppermute | solution.py:525
  54.7 1.4 %collective-permute-start.7 = (bf16[160,1024]{1,0:T(8,128)(2,1)S(1)}, bf16[160,1024]{1,0:T(8,128)(2,1)S(1)}, u32[]{:S(2)}, u32[]{:S(2)}) collective-permute-start(bf16[160,1024]{1,0:T(8,128)(2,1)S(1)} %get-tuple-element.65), channel_id=1, source_target_pairs={{0,12},{4,0},{8,4},{12,8},{16,28},{20,16},{24,20},{28,24},{1,13},{... | collective-permute-start | bytes 983048 | tf_op jit(solution)/shard_map/ppermute | solution.py:525
  56.1 1.6 %collective-permute-start.3 = (bf16[128,1024]{1,0:T(8,128)(2,1)S(1)}, bf16[128,1024]{1,0:T(8,128)(2,1)S(1)}, u32[]{:S(2)}, u32[]{:S(2)}) collective-permute-start(bf16[128,1024]{1,0:T(8,128)(2,1)S(1)} %bitcast.26), channel_id=1, source_target_pairs={{0,16},{4,20},{8,24},{12,28},{16,0},{20,4},{24,8},{28,12},{1,17},{... | collective-permute-start | bytes 786440 | tf_op jit(solution)/shard_map/ppermute | solution.py:520
  57.8 3.7 %shard_map.106 = (bf16[2,256,1024]{2,1,0:T(8,128)(2,1)S(1)}, bf16[2,256,1024]{2,1,0:T(8,128)(2,1)S(1)}) custom-call(s32[1]{0:T(128)} %bitcast.9.core_ref, bf16[256,1024]{1,0:T(8,128)(2,1)S(1)} %shard_map.102.refs_1_.a_ref, bf16[1024,4096]{1,0:T(8,128)(2,1)S(1)} %bitcast.20), custom_call_target="tpu_custom_call" | custom-call | flops 1024 | bytes 1024 | tf_op jit(solution)/shard_map/pallas_call | solution.py:267
  61.5 12.5 %collective-permute-done.3.refs_2_ = bf16[128,1024]{1,0:T(8,128)(2,1)S(1)} collective-permute-done((bf16[128,1024]{1,0:T(8,128)(2,1)S(1)}, bf16[128,1024]{1,0:T(8,128)(2,1)S(1)}, u32[]{:S(2)}, u32[]{:S(2)}) %collective-permute-start.3) | collective-permute-done | bytes 262176 | tf_op jit(solution)/shard_map/ppermute | solution.py:520
  74.0 0.0 collective-permute-start.10
  74.0 0.0 collective-permute-done.4.refs_5_
  74.0 0.0 collective-permute-done.5.refs_3_
  74.0 0.0 collective-permute-done.6.refs_4_
  74.0 0.0 collective-permute-done.7.refs_5_
  74.0 1.7 %shard_map.105 = f32[640,128]{1,0:T(8,128)S(1)} custom-call(bf16[256,1024]{1,0:T(8,128)(2,1)S(1)} %bitcast.25, bf16[256,1024]{1,0:T(8,128)(2,1)} %collective-permute-done.refs_1_, bf16[160,1024]{1,0:T(8,128)(2,1)S(1)} %get-tuple-element.62.refs_2_, bf16[160,1024]{1,0:T(8,128)(2,1)S(1)} %collective-permute-done.5.refs_3_, ...), custom_call_target="tpu_custom_call" | custom-call | flops 8589934592 | bytes 16777216 | tf_op jit(solution)/shard_map/pallas_call | solution.py:363
  75.7 0.5 collective-permute-start.8
  76.3 1.3 %collective-permute-done.8 = f32[640,128]{1,0:T(8,128)S(1)} collective-permute-done((f32[640,128]{1,0:T(8,128)S(1)}, f32[640,128]{1,0:T(8,128)S(1)}, u32[]{:S(2)}, u32[]{:S(2)}) %collective-permute-start.8) | collective-permute-done | bytes 327712 | tf_op jit(solution)/shard_map/ppermute | solution.py:531
  77.6 0.6 collective-permute-start.9
  78.2 0.0 collective-permute-done.10.come_ref
  78.2 1.0 shard_map.107
  79.1 5.0 %collective-permute-done.9.refs_4_ = bf16[640,128]{1,0:T(8,128)(2,1)S(1)} collective-permute-done((bf16[640,128]{1,0:T(8,128)(2,1)S(1)}, bf16[640,128]{1,0:T(8,128)(2,1)S(1)}, u32[]{:S(2)}, u32[]{:S(2)}) %collective-permute-start.9) | collective-permute-done | bytes 163872 | tf_op jit(solution)/shard_map/ppermute | solution.py:533
  84.1 0.5 collective-permute-start.14
  84.6 1.5 %shard_map.108 = (bf16[160,1024]{1,0:T(8,128)(2,1)S(1)}, bf16[160,1024]{1,0:T(8,128)(2,1)}, bf16[160,1024]{1,0:T(8,128)(2,1)}, bf16[160,1024]{1,0:T(8,128)(2,1)}) custom-call(bf16[256,1024]{1,0:T(8,128)(2,1)S(1)} %bitcast.21, bf16[128,1024]{1,0:T(8,128)(2,1)S(1)} %collective-permute-done.1.refs_1_, bf16[128,1024]{1,0:T(8,128)(2,1)S(1)} %collective-permute-done.3.refs_2_, ...), custom_call_target="tpu_custom_call" | custom-call | flops 1024 | bytes 1024 | tf_op jit(solution)/shard_map/pallas_call | solution.py:403
  86.1 2.4 %collective-permute-start.11 = (bf16[160,1024]{1,0:T(8,128)(2,1)}, bf16[160,1024]{1,0:T(8,128)(2,1)S(1)}, u32[]{:S(2)}, u32[]{:S(2)}) collective-permute-start(bf16[160,1024]{1,0:T(8,128)(2,1)} %get-tuple-element.74), channel_id=1, source_target_pairs={{0,12},{4,0},{8,4},{12,8},{16,28},{20,16},{24,20},{28,24},{1,13},{... | collective-permute-start | bytes 983048 | tf_op jit(solution)/shard_map/ppermute | solution.py:538
  88.5 1.0 collective-permute-start.12
  89.5 1.4 %collective-permute-start.13 = (bf16[160,1024]{1,0:T(8,128)(2,1)}, bf16[160,1024]{1,0:T(8,128)(2,1)}, u32[]{:S(2)}, u32[]{:S(2)}) collective-permute-start(bf16[160,1024]{1,0:T(8,128)(2,1)} %get-tuple-element.76), channel_id=1, source_target_pairs={{0,4},{4,8},{8,12},{12,0},{16,20},{20,24},{24,28},{28,16},{1,5},{5... | collective-permute-start | bytes 983048 | tf_op jit(solution)/shard_map/ppermute | solution.py:538
  90.9 0.1 copy.12.target_ref
  91.1 5.9 %collective-permute-done.11.refs_1_ = bf16[160,1024]{1,0:T(8,128)(2,1)S(1)} collective-permute-done((bf16[160,1024]{1,0:T(8,128)(2,1)}, bf16[160,1024]{1,0:T(8,128)(2,1)S(1)}, u32[]{:S(2)}, u32[]{:S(2)}) %collective-permute-start.11) | collective-permute-done | bytes 327712 | tf_op jit(solution)/shard_map/ppermute | solution.py:538
  97.0 0.7 copy-done.6
  97.7 5.8 %collective-permute-done.12.refs_2_ = bf16[160,1024]{1,0:T(8,128)(2,1)} collective-permute-done((bf16[160,1024]{1,0:T(8,128)(2,1)}, bf16[160,1024]{1,0:T(8,128)(2,1)}, u32[]{:S(2)}, u32[]{:S(2)}) %collective-permute-start.12) | collective-permute-done | bytes 327712 | tf_op jit(solution)/shard_map/ppermute | solution.py:538
  103.5 1.1 collective-permute-done.13.refs_3_
  104.6 0.0 collective-permute-done.14.refs_7_
  104.6 0.8 copy-done.4
  105.4 1.0 copy-done.5
  106.4 1.0 copy-done.7
  107.4 2.4 %shard_map.109 = bf16[512,1024]{1,0:T(8,128)(2,1)S(1)} custom-call(s32[512,1]{1,0:T(8,128)S(1)} %copy.12.target_ref, bf16[160,1024]{1,0:T(8,128)(2,1)S(1)} %get-tuple-element.73.refs_0_, bf16[160,1024]{1,0:T(8,128)(2,1)S(1)} %copy-done.7, bf16[160,1024]{1,0:T(8,128)(2,1)} %collective-permute-done.12.refs_2_, ...), custom_call_target="tpu_custom_call" | custom-call | flops 1024 | bytes 1024 | tf_op jit(solution)/shard_map/pallas_call | solution.py:438
  109.8 1.2 %reshape.36 = bf16[128,4,1024]{2,1,0:T(4,128)(2,1)} reshape(bf16[512,1024]{1,0:T(8,128)(2,1)S(1)} %shard_map.109) | data formatting | bytes 2097152 | tf_op jit(solution)/shard_map/reshape | solution.py:542
  (20 shorter events, 0.1 us)
Async XLA Ops:
  0.0 32.5 %collective-permute-start = (bf16[256,1024]{1,0:T(8,128)(2,1)}, bf16[256,1024]{1,0:T(8,128)(2,1)}, u32[]{:S(2)}, u32[]{:S(2)}) collective-permute-start(bf16[256,1024]{1,0:T(8,128)(2,1)} %bitcast.24), channel_id=1, source_target_pairs={{0,16},{4,20},{8,24},{12,28},{16,0},{20,4},{24,8},{28,12},{1,17},{... | collective-permute-start | bytes 1572872 | tf_op jit(solution)/shard_map/ppermute | solution.py:511
  10.8 2.2 %copy-start.8 = (bf16[2,2,2048,256]{3,2,1,0:T(8,128)(2,1)S(1)}, bf16[2,2,2048,256]{3,2,1,0:T(8,128)(2,1)}, u32[]{:S(2)}) copy-start(bf16[2,2,2048,256]{3,2,1,0:T(8,128)(2,1)} %kv_ref.3) | copy-start | bytes 12582916
  13.0 2.2 %copy-start.10 = (bf16[2,128,32,256]{3,2,1,0:T(8,128)(2,1)S(1)}, bf16[2,128,32,256]{3,2,1,0:T(8,128)(2,1)}, u32[]{:S(2)}) copy-start(bf16[2,128,32,256]{3,2,1,0:T(8,128)(2,1)} %suf_ref.3) | copy-start | bytes 12582916
  15.2 9.4 %copy-start.2 = (bf16[512,1024]{1,0:T(8,128)(2,1)}, bf16[512,1024]{1,0:T(8,128)(2,1)S(1)}, u32[]{:S(2)}) copy-start(bf16[512,1024]{1,0:T(8,128)(2,1)S(1)} %reshape.33.q_ref) | copy-start | bytes 3145732
  24.6 3.4 %copy-start = (bf16[1024,4096]{1,0:T(8,128)(2,1)S(1)}, bf16[1024,4096]{1,0:T(8,128)(2,1)}, u32[]{:S(2)}) copy-start(bf16[1024,4096]{1,0:T(8,128)(2,1)} %w_ref.3) | copy-start | bytes 25165828
  32.5 16.0 %collective-permute-start.2 = (bf16[2,256,1024]{2,1,0:T(8,128)(2,1)}, bf16[2,256,1024]{2,1,0:T(8,128)(2,1)S(1)}, u32[]{:S(2)}, u32[]{:S(2)}) collective-permute-start(bf16[2,256,1024]{2,1,0:T(8,128)(2,1)} %get-tuple-element.51), channel_id=1, source_target_pairs={{0,1},{1,0},{2,3},{3,2},{4,5},{5,4},{6,7},{7,6},{8,9},{9,8},{10,11... | collective-permute-start | bytes 3145736 | tf_op jit(solution)/shard_map/ppermute | solution.py:514
  32.5 25.3 %slice-start = ((s8[8388608]{0:T(1024)(128)(4,1)}), s8[4194304]{0:T(1024)(128)(4,1)S(1)}, s32[]{:S(2)}) async-start(s8[8388608]{0:T(1024)(128)(4,1)} %bitcast.19), calls=%async_computation | async-start | bytes 8388608
  32.5 25.3 %slice-start.1 = ((s8[8388608]{0:T(1024)(128)(4,1)}), s8[4194304]{0:T(1024)(128)(4,1)S(1)}, s32[]{:S(2)}) async-start(s8[8388608]{0:T(1024)(128)(4,1)} %bitcast.19), calls=%async_computation.1 | async-start | bytes 8388608
  32.5 16.2 %collective-permute-start.1 = (bf16[128,1024]{1,0:T(8,128)(2,1)S(1)}, bf16[128,1024]{1,0:T(8,128)(2,1)S(1)}, u32[]{:S(2)}, u32[]{:S(2)}) collective-permute-start(bf16[128,1024]{1,0:T(8,128)(2,1)S(1)} %bitcast.27), channel_id=1, source_target_pairs={{0,16},{4,20},{8,24},{12,28},{16,0},{20,4},{24,8},{28,12},{1,17},{... | collective-permute-start | bytes 786440 | tf_op jit(solution)/shard_map/ppermute | solution.py:516
  32.6 1.4 %copy-start.3 = (bf16[512,1024]{1,0:T(8,128)(2,1)S(1)}, bf16[512,1024]{1,0:T(8,128)(2,1)}, u32[]{:S(2)}) copy-start(bf16[512,1024]{1,0:T(8,128)(2,1)} %copy-done.2) | copy-start | bytes 3145732
  34.0 2.9 %copy-start.9 = (bf16[2,2,2048,256]{3,2,1,0:T(8,128)(2,1)S(1)}, bf16[2,2,2048,256]{3,2,1,0:T(8,128)(2,1)}, u32[]{:S(2)}) copy-start(bf16[2,2,2048,256]{3,2,1,0:T(8,128)(2,1)} %kv_ref.3) | copy-start | bytes 12582916
  36.9 2.2 %copy-start.11 = (bf16[2,128,32,256]{3,2,1,0:T(8,128)(2,1)S(1)}, bf16[2,128,32,256]{3,2,1,0:T(8,128)(2,1)}, u32[]{:S(2)}) copy-start(bf16[2,128,32,256]{3,2,1,0:T(8,128)(2,1)} %suf_ref.3) | copy-start | bytes 12582916
  39.0 17.1 %copy-start.13 = (bf16[2,64,1024]{2,1,0:T(8,128)(2,1)S(1)}, bf16[2,64,1024]{2,1,0:T(8,128)(2,1)}, u32[]{:S(2)}) copy-start(bf16[2,64,1024]{2,1,0:T(8,128)(2,1)} %get-tuple-element.81) | copy-start | bytes 786436
  48.7 25.3 %collective-permute-start.4 = (bf16[256,1024]{1,0:T(8,128)(2,1)S(1)}, bf16[256,1024]{1,0:T(8,128)(2,1)S(1)}, u32[]{:S(2)}, u32[]{:S(2)}) collective-permute-start(bf16[256,1024]{1,0:T(8,128)(2,1)S(1)} %get-tuple-element.59), channel_id=1, source_target_pairs={{0,2},{1,3},{2,0},{3,1},{4,6},{5,7},{6,4},{7,5},{8,10},{9,11},{10,... | collective-permute-start | bytes 1572872 | tf_op jit(solution)/shard_map/ppermute | solution.py:508
  51.6 22.4 %collective-permute-start.5 = (bf16[160,1024]{1,0:T(8,128)(2,1)S(1)}, bf16[160,1024]{1,0:T(8,128)(2,1)S(1)}, u32[]{:S(2)}, u32[]{:S(2)}) collective-permute-start(bf16[160,1024]{1,0:T(8,128)(2,1)S(1)} %get-tuple-element.63), channel_id=1, source_target_pairs={{0,4},{4,8},{8,12},{12,0},{16,20},{20,24},{24,28},{28,16},{1,5},{5... | collective-permute-start | bytes 983048 | tf_op jit(solution)/shard_map/ppermute | solution.py:525
  53.2 20.8 %collective-permute-start.6 = (bf16[160,1024]{1,0:T(8,128)(2,1)S(1)}, bf16[160,1024]{1,0:T(8,128)(2,1)S(1)}, u32[]{:S(2)}, u32[]{:S(2)}) collective-permute-start(bf16[160,1024]{1,0:T(8,128)(2,1)S(1)} %get-tuple-element.64), channel_id=1, source_target_pairs={{0,8},{4,12},{8,0},{12,4},{16,24},{20,28},{24,16},{28,20},{1,9},{5... | collective-permute-start | bytes 983048 | tf_op jit(solution)/shard_map/ppermute | solution.py:525
  54.7 19.3 %collective-permute-start.7 = (bf16[160,1024]{1,0:T(8,128)(2,1)S(1)}, bf16[160,1024]{1,0:T(8,128)(2,1)S(1)}, u32[]{:S(2)}, u32[]{:S(2)}) collective-permute-start(bf16[160,1024]{1,0:T(8,128)(2,1)S(1)} %get-tuple-element.65), channel_id=1, source_target_pairs={{0,12},{4,0},{8,4},{12,8},{16,28},{20,16},{24,20},{28,24},{1,13},{... | collective-permute-start | bytes 983048 | tf_op jit(solution)/shard_map/ppermute | solution.py:525
  56.1 17.8 %collective-permute-start.3 = (bf16[128,1024]{1,0:T(8,128)(2,1)S(1)}, bf16[128,1024]{1,0:T(8,128)(2,1)S(1)}, u32[]{:S(2)}, u32[]{:S(2)}) collective-permute-start(bf16[128,1024]{1,0:T(8,128)(2,1)S(1)} %bitcast.26), channel_id=1, source_target_pairs={{0,16},{4,20},{8,24},{12,28},{16,0},{20,4},{24,8},{28,12},{1,17},{... | collective-permute-start | bytes 786440 | tf_op jit(solution)/shard_map/ppermute | solution.py:520
  57.8 16.2 %copy-start.12 = (bf16[4,64,1024]{2,1,0:T(8,128)(2,1)S(1)}, bf16[4,64,1024]{2,1,0:T(8,128)(2,1)}, u32[]{:S(2)}) copy-start(bf16[4,64,1024]{2,1,0:T(8,128)(2,1)} %param.18) | copy-start | bytes 1572868
  74.0 10.6 %copy-start.1 = (bf16[4,64,1024]{2,1,0:T(8,128)(2,1)S(1)}, bf16[4,64,1024]{2,1,0:T(8,128)(2,1)}, u32[]{:S(2)}) copy-start(bf16[4,64,1024]{2,1,0:T(8,128)(2,1)} %param.19) | copy-start | bytes 1572868
  74.0 4.2 %collective-permute-start.10 = (bf16[2,256,1024]{2,1,0:T(8,128)(2,1)S(1)}, bf16[2,256,1024]{2,1,0:T(8,128)(2,1)S(1)}, u32[]{:S(2)}, u32[]{:S(2)}) collective-permute-start(bf16[2,256,1024]{2,1,0:T(8,128)(2,1)S(1)} %get-tuple-element.68), channel_id=1, source_target_pairs={{0,1},{1,0},{2,3},{3,2},{4,5},{5,4},{6,7},{7,6},{8,9},{9,8},{10,11... | collective-permute-start | bytes 3145736 | tf_op jit(solution)/shard_map/ppermute | solution.py:528
  75.7 1.8 %collective-permute-start.8 = (f32[640,128]{1,0:T(8,128)S(1)}, f32[640,128]{1,0:T(8,128)S(1)}, u32[]{:S(2)}, u32[]{:S(2)}) collective-permute-start(f32[640,128]{1,0:T(8,128)S(1)} %shard_map.105), channel_id=1, source_target_pairs={{0,1},{1,0},{2,3},{3,2},{4,5},{5,4},{6,7},{7,6},{8,9},{9,8},{10,11... | collective-permute-start | bytes 983048 | tf_op jit(solution)/shard_map/ppermute | solution.py:531
  77.6 6.5 %collective-permute-start.9 = (bf16[640,128]{1,0:T(8,128)(2,1)S(1)}, bf16[640,128]{1,0:T(8,128)(2,1)S(1)}, u32[]{:S(2)}, u32[]{:S(2)}) collective-permute-start(bf16[640,128]{1,0:T(8,128)(2,1)S(1)} %add_convert_fusion.refs_3_), channel_id=1, source_target_pairs={{0,2},{1,3},{2,0},{3,1},{4,6},{5,7},{6,4},{7,5},{8,10},{9,11},{10,... | collective-permute-start | bytes 491528 | tf_op jit(solution)/shard_map/ppermute | solution.py:533
  84.1 20.5 %collective-permute-start.14 = (bf16[256,1024]{1,0:T(8,128)(2,1)}, bf16[256,1024]{1,0:T(8,128)(2,1)S(1)}, u32[]{:S(2)}, u32[]{:S(2)}) collective-permute-start(bf16[256,1024]{1,0:T(8,128)(2,1)} %get-tuple-element.80), channel_id=1, source_target_pairs={{0,2},{1,3},{2,0},{3,1},{4,6},{5,7},{6,4},{7,5},{8,10},{9,11},{10,... | collective-permute-start | bytes 1572872 | tf_op jit(solution)/shard_map/ppermute | solution.py:508
  86.1 10.9 %collective-permute-start.11 = (bf16[160,1024]{1,0:T(8,128)(2,1)}, bf16[160,1024]{1,0:T(8,128)(2,1)S(1)}, u32[]{:S(2)}, u32[]{:S(2)}) collective-permute-start(bf16[160,1024]{1,0:T(8,128)(2,1)} %get-tuple-element.74), channel_id=1, source_target_pairs={{0,12},{4,0},{8,4},{12,8},{16,28},{20,16},{24,20},{28,24},{1,13},{... | collective-permute-start | bytes 983048 | tf_op jit(solution)/shard_map/ppermute | solution.py:538
  88.5 15.0 %collective-permute-start.12 = (bf16[160,1024]{1,0:T(8,128)(2,1)}, bf16[160,1024]{1,0:T(8,128)(2,1)}, u32[]{:S(2)}, u32[]{:S(2)}) collective-permute-start(bf16[160,1024]{1,0:T(8,128)(2,1)} %get-tuple-element.75), channel_id=1, source_target_pairs={{0,8},{4,12},{8,0},{12,4},{16,24},{20,28},{24,16},{28,20},{1,9},{5... | collective-permute-start | bytes 983048 | tf_op jit(solution)/shard_map/ppermute | solution.py:538
  89.5 15.0 %collective-permute-start.13 = (bf16[160,1024]{1,0:T(8,128)(2,1)}, bf16[160,1024]{1,0:T(8,128)(2,1)}, u32[]{:S(2)}, u32[]{:S(2)}) collective-permute-start(bf16[160,1024]{1,0:T(8,128)(2,1)} %get-tuple-element.76), channel_id=1, source_target_pairs={{0,4},{4,8},{8,12},{12,0},{16,20},{20,24},{24,28},{28,16},{1,5},{5... | collective-permute-start | bytes 983048 | tf_op jit(solution)/shard_map/ppermute | solution.py:538
  97.0 0.7 copy-start.6
  104.6 0.8 copy-start.4
  105.4 1.0 copy-start.5
  106.4 1.0 copy-start.7

commit v2 on v1

--- a/solution.py
+++ b/solution.py
@@ -11,8 +11,7 @@
 HEAD_SIZE = 128
 MOST = 5
 FOLD = 2
-CUTS = 2
-PARTS = 2
+CUTS = 1
 BLOCK_ROLLS = 16
 KEY_CHUNK = 512
 NEG = float("-inf")
@@ -20,6 +19,8 @@
 BRIEF = pl.CostEstimate(flops=1024, bytes_accessed=1024, transcendentals=0)
 LENGTHY = pl.CostEstimate(flops=1 << 33, bytes_accessed=1 << 24, transcendentals=0)
 VMEM = pl.BlockSpec(memory_space=pltpu.VMEM)
+ANY = pl.BlockSpec(memory_space=pl.ANY)
+SMEM = pl.BlockSpec(memory_space=pltpu.SMEM)
 
 
 def dot_nt(a, b):
@@ -31,11 +32,13 @@
 
 
 def attend_kernel(
-    code_ref, q_ref, kv_ref, suf_ref, fr_ref, o_ref, s_ref, m_ref, *, steps, group, first, blocks
+    length_ref, prefix_ref, q_ref, kv_hbm, suf_hbm, fr_ref, o_ref,
+    s_ref, m_ref, kv_ref, suf_ref, sems,
+    *, steps, group, first, blocks
 ):
     prefix_count, prefix_len = kv_ref.shape[1], kv_ref.shape[2]
     key_heads = kv_ref.shape[3] // HEAD_SIZE
-    rolls, suf_len = suf_ref.shape[1], suf_ref.shape[2]
+    rolls, suf_len = suf_hbm.shape[1], suf_hbm.shape[2]
     block_rows = BLOCK_ROLLS * steps
     rows = block_rows * group
     last = first + blocks - 1
@@ -52,10 +55,21 @@
         shape = (block_rows, rolls)
         mine = block * BLOCK_ROLLS + lax.broadcasted_iota(jnp.int32, shape, 0) // steps
         lane = lax.broadcasted_iota(jnp.int32, shape, 1)
-        code = jnp.broadcast_to(code_ref[...].astype(jnp.float32), shape)
+        code = length_ref[...] * prefix_count + prefix_ref[...] % prefix_count
+        code = jnp.broadcast_to(code.astype(jnp.float32), shape)
         col = jnp.sum(jnp.where(mine == lane, code, 0.0), axis=1, keepdims=True)
         col = jnp.broadcast_to(col, (block_rows, HEAD_SIZE)).astype(jnp.int32)
         return col // prefix_count, col % prefix_count
+
+    mine = pl.ds(first * BLOCK_ROLLS, blocks * BLOCK_ROLLS)
+    loads = []
+    for which in range(2):
+        loads.append(pltpu.make_async_copy(kv_hbm.at[which], kv_ref.at[which], sems.at[2 * which]))
+        loads.append(
+            pltpu.make_async_copy(suf_hbm.at[which, mine], suf_ref.at[which], sems.at[2 * which + 1])
+        )
+    for load in loads:
+        load.start()
 
     def tile_rows(x):
         return jnp.concatenate([x] * group, axis=0)
@@ -71,7 +85,7 @@
         return pl.ds(h * HEAD_SIZE, HEAD_SIZE)
 
     def suffix_tile(which, block, i, h):
-        start = block * BLOCK_ROLLS + i * suf_rolls
+        start = (block - first) * BLOCK_ROLLS + i * suf_rolls
         tile = suf_ref[which, pl.ds(start, suf_rolls), :, head_lanes(h)]
         return tile.reshape(HEAD_SIZE, HEAD_SIZE)
 
@@ -201,7 +215,11 @@
             for stream in streams:
                 next(stream)
 
+    for load in loads[:2]:
+        load.wait()
     run(scores(first, 0, 0))
+    for load in loads[2:]:
+        load.wait()
 
     def body(block, carry):
         for h in range(key_heads):
@@ -218,28 +236,29 @@
     lax.fori_loop(first, first + blocks, body, 0)
 
 
-def attend(code, queries, prefix, suffix, fresh, steps, part):
-    rows, width = queries.shape
-    rows = rows // PARTS
+def attend(lengths, prefixes, queries, prefix, suffix, fresh, steps, first, blocks):
+    width = queries.shape[-1]
+    rows = blocks * BLOCK_ROLLS * steps
     key_heads = prefix.shape[3] // HEAD_SIZE
     group = width // HEAD_SIZE // key_heads
     unit_rows = BLOCK_ROLLS * steps * group
     span = prefix.shape[2] + 2 * HEAD_SIZE
-    blocks = suffix.shape[1] // BLOCK_ROLLS // PARTS
+    held = (2, blocks * BLOCK_ROLLS) + suffix.shape[2:]
     return pl.pallas_call(
-        functools.partial(
-            attend_kernel, steps=steps, group=group, first=part * blocks, blocks=blocks
-        ),
+        functools.partial(attend_kernel, steps=steps, group=group, first=first, blocks=blocks),
         out_shape=jax.ShapeDtypeStruct((rows, width), jnp.bfloat16),
-        in_specs=[VMEM] * 5,
+        in_specs=[VMEM, VMEM, VMEM, ANY, ANY, VMEM],
         out_specs=VMEM,
         scratch_shapes=[
             pltpu.VMEM((key_heads, unit_rows, span), jnp.float32),
             pltpu.VMEM((key_heads, unit_rows, HEAD_SIZE), jnp.float32),
+            pltpu.VMEM(prefix.shape, prefix.dtype),
+            pltpu.VMEM(held, suffix.dtype),
+            pltpu.SemaphoreType.DMA((4,)),
         ],
-        compiler_params=pltpu.CompilerParams(vmem_limit_bytes=20 * MIB),
+        compiler_params=pltpu.CompilerParams(vmem_limit_bytes=52 * MIB),
         cost_estimate=LENGTHY,
-    )(code, queries, prefix, suffix, fresh)
+    )(lengths, prefixes, queries, prefix, suffix, fresh)
 
 
 def project_kernel(core_ref, a_ref, w_ref, send_ref, keep_ref, *, count):
@@ -284,50 +303,101 @@
     )(core, attended, weight)
 
 
-def pair_kernel(chip_ref, keep_ref, come_ref, *outs):
-    chips = len(outs)
-    for shift, out in enumerate(outs):
+def pair_kernel(chip_ref, keep_ref, come_ref, own_ref, *outs, cuts):
+    chips = keep_ref.shape[0]
+    for shift in range(chips):
         index = (chip_ref[0] + shift) % chips
         pair = keep_ref[index].astype(jnp.float32) + come_ref[index].astype(jnp.float32)
-        out[...] = pair.astype(jnp.bfloat16)
-
-
-def pair_sums(chip, keep, come):
+        pair = pair.astype(jnp.bfloat16)
+        if shift == 0:
+            own_ref[...] = pair
+        else:
+            for k in range(cuts):
+                out = outs[(shift - 1) * cuts + k]
+                rows = out.shape[0]
+                out[...] = pair[k * rows : (k + 1) * rows]
+
+
+def pair_sums(chip, keep, come, cuts):
     chips, rows, width = keep.shape
+    away = [jax.ShapeDtypeStruct((rows // cuts, width), jnp.bfloat16)] * ((chips - 1) * cuts)
     return pl.pallas_call(
-        pair_kernel,
-        out_shape=[jax.ShapeDtypeStruct((rows, width), jnp.bfloat16)] * chips,
-        in_specs=[pl.BlockSpec(memory_space=pltpu.SMEM), VMEM, VMEM],
-        out_specs=[VMEM] * chips,
-        compiler_params=pltpu.CompilerParams(vmem_limit_bytes=8 * MIB),
+        functools.partial(pair_kernel, cuts=cuts),
+        out_shape=[jax.ShapeDtypeStruct((rows, width), jnp.bfloat16)] + away,
+        in_specs=[SMEM, VMEM, VMEM],
+        out_specs=[VMEM] * (1 + len(away)),
+        compiler_params=pltpu.CompilerParams(vmem_limit_bytes=12 * MIB),
         cost_estimate=BRIEF,
     )(chip, keep, come)
 
 
-def pack_kernel(target_ref, *refs):
-    parts, outs = refs[:PARTS], refs[PARTS:]
-    slots = outs[0].shape[0]
-    part_rows = parts[0].shape[0]
+def slot_of(row, turn, here, resident, holders):
+    block = holders // FOLD
+    holder = row // resident
+    fold = (here // block - holder // block + FOLD) % FOLD
+    place = (holder % block - here % block + block) % block
+    return ((place * FOLD + fold) * resident + row % resident) * MOST + turn
+
+
+def row_slots(row_ref, here, resident, holders):
+    row = row_ref[...]
+    shape = (row.shape[1], row.shape[1])
+    across = jnp.broadcast_to(row, shape)
+    down, lane = lax.broadcasted_iota(jnp.int32, shape, 0), lax.broadcasted_iota(jnp.int32, shape, 1)
+    values = across.astype(jnp.float32)
+    col = jnp.sum(jnp.where(down == lane, values, 0.0), axis=1, keepdims=True)
+    same = jnp.broadcast_to(col, shape) == values
+    turn_row = jnp.sum(jnp.where(same & (down < lane), 1.0, 0.0), axis=0, keepdims=True)
+    turn_col = jnp.sum(jnp.where(same & (lane < down), 1.0, 0.0), axis=1, keepdims=True)
+    place_row = slot_of(row, turn_row.astype(jnp.int32), here, resident, holders)
+    place_col = slot_of(
+        jnp.broadcast_to(col, shape).astype(jnp.int32),
+        jnp.broadcast_to(turn_col, shape).astype(jnp.int32),
+        here,
+        resident,
+        holders,
+    )
+    return place_row, place_col[:, :1]
+
+
+def pack_kernel(here_ref, row_ref, *refs, steps, resident, holders, count):
+    parts, outs = refs[:-count], refs[-count:]
+    slots, rolls = outs[0].shape[0], row_ref.shape[1]
+    place, _ = row_slots(row_ref, here_ref[0], resident, holders)
     for d, out in enumerate(outs):
-        total = None
-        for k, part in enumerate(parts):
-            row = d * slots + lax.broadcasted_iota(jnp.int32, (slots, part_rows), 0)
-            chosen = row == target_ref[:, k * part_rows : (k + 1) * part_rows]
-            term = dot_nn(jnp.where(chosen, 1.0, 0.0).astype(jnp.bfloat16), part[...])
+        shape = (slots, rolls)
+        slot = (d * slots + lax.broadcasted_iota(jnp.int32, shape, 0)) // steps
+        picked = jnp.where(slot == jnp.broadcast_to(place, shape), 1.0, 0.0).astype(jnp.bfloat16)
+        total, start = None, 0
+        for part in parts:
+            rows = part.shape[0]
+            shape = (rolls, rows)
+            spread = lax.broadcasted_iota(jnp.int32, shape, 0) == (
+                start + lax.broadcasted_iota(jnp.int32, shape, 1)
+            ) // steps
+            chosen = dot_nn(picked, jnp.where(spread, 1.0, 0.0).astype(jnp.bfloat16))
+            shape = (slots, rows)
+            step = lax.broadcasted_iota(jnp.int32, shape, 0) % steps
+            aligned = step == (start + lax.broadcasted_iota(jnp.int32, shape, 1)) % steps
+            chosen = jnp.where(aligned, chosen, 0.0).astype(jnp.bfloat16)
+            term = dot_nn(chosen, part[...])
             total = term if total is None else total + term
+            start += rows
         out[...] = total.astype(jnp.bfloat16)
 
 
-def pack(target, parts, count, slots):
-    rows, width = parts[0].shape
+def pack(here, adapter_row, parts, count, slots, steps, resident, holders):
+    width = parts[0].shape[1]
     return pl.pallas_call(
-        pack_kernel,
+        functools.partial(
+            pack_kernel, steps=steps, resident=resident, holders=holders, count=count
+        ),
         out_shape=[jax.ShapeDtypeStruct((slots, width), jnp.bfloat16)] * count,
-        in_specs=[VMEM] * (1 + len(parts)),
+        in_specs=[SMEM] + [VMEM] * (1 + len(parts)),
         out_specs=[VMEM] * count,
-        compiler_params=pltpu.CompilerParams(vmem_limit_bytes=8 * MIB),
+        compiler_params=pltpu.CompilerParams(vmem_limit_bytes=12 * MIB),
         cost_estimate=BRIEF,
-    )(target, *parts)
+    )(here, adapter_row, *parts)
 
 
 def adapter_mask(rows, per_adapter, rank, tile):
@@ -339,6 +409,7 @@
 def shrink_kernel(*refs, per_adapter, rank, count):
     weights, pieces, out = refs[:FOLD], refs[FOLD : FOLD + count], refs[-1]
     rows = pieces[0].shape[0] // FOLD
+    found = []
     for k in range(FOLD):
         span = pl.ds(k * rows, rows)
         every = dot_nt(
@@ -354,7 +425,11 @@
             summed = total
             for turn in range(1, HEAD_SIZE // rank):
                 summed = summed + pltpu.roll(total, turn * rank, axis=1)
-            out[pl.ds((d * FOLD + k) * rows, rows), :] = summed
+            found.append(summed)
+    lane = lax.broadcasted_iota(jnp.int32, (rows, HEAD_SIZE), 1)
+    for d in range(count):
+        both = jnp.where(lane < rank, found[d], found[count + d])
+        out[pl.ds(d * rows, rows), :] = both
 
 
 def shrink_rows(weights, pieces, per_adapter, rank):
@@ -362,7 +437,7 @@
     rows, width = pieces[0].shape
     return pl.pallas_call(
         functools.partial(shrink_kernel, per_adapter=per_adapter, rank=rank, count=count),
-        out_shape=jax.ShapeDtypeStruct((count * rows, HEAD_SIZE), jnp.float32),
+        out_shape=jax.ShapeDtypeStruct((count * rows // FOLD, HEAD_SIZE), jnp.float32),
         in_specs=[VMEM] * (FOLD + count),
         out_specs=VMEM,
         compiler_params=pltpu.CompilerParams(vmem_limit_bytes=8 * MIB),
@@ -371,17 +446,19 @@
 
 
 def expand_kernel(*refs, per_adapter, rank, count, terms):
-    own, sums, outs = refs[0], refs[1 + CUTS : 1 + CUTS + terms], refs[1 + CUTS + terms :]
-    weights = [own[...], jnp.concatenate([x[...] for x in refs[1 : 1 + CUTS]], axis=0)]
-    depth = own.shape[0]
+    weights, sums, outs = refs[:FOLD], refs[FOLD : FOLD + terms], refs[FOLD + terms :]
+    depth = weights[0].shape[0]
     rows = outs[0].shape[0] // FOLD
     for k in range(FOLD):
         spread = []
         for d in range(count):
-            span = pl.ds((d * FOLD + k) * rows, rows)
+            span = pl.ds(d * rows, rows)
             code = sums[0][span, :].astype(jnp.float32)
             for other in sums[1:]:
                 code = code + other[span, :].astype(jnp.float32)
+            lane = lax.broadcasted_iota(jnp.int32, (rows, HEAD_SIZE), 1)
+            turned = pltpu.roll(code, rank, axis=1)
+            code = jnp.where((lane < rank) == (k == 0), code, turned)
             spread.append(
                 jnp.concatenate(
                     [
@@ -391,58 +468,87 @@
                     axis=1,
                 ).astype(jnp.bfloat16)
             )
-        wide = dot_nn(jnp.concatenate(spread, axis=0), weights[k])
+        wide = dot_nn(jnp.concatenate(spread, axis=0), weights[k][...])
         wide = wide.astype(jnp.bfloat16)
         for d in range(count):
             outs[d][pl.ds(k * rows, rows), :] = wide[d * rows : (d + 1) * rows]
 
 
 def expand_rows(weights, sums, per_adapter, rank, count):
-    rows = sums[0].shape[0] // count
+    rows = sums[0].shape[0] // count * FOLD
     width = weights[0].shape[1]
     return pl.pallas_call(
         functools.partial(
             expand_kernel, per_adapter=per_adapter, rank=rank, count=count, terms=len(sums)
         ),
         out_shape=[jax.ShapeDtypeStruct((rows, width), jnp.bfloat16)] * count,
-        in_specs=[VMEM] * (1 + CUTS + len(sums)),
+        in_specs=[VMEM] * (FOLD + len(sums)),
         out_specs=[VMEM] * count,
         compiler_params=pltpu.CompilerParams(vmem_limit_bytes=8 * MIB),
         cost_estimate=BRIEF,
     )(*weights, *sums)
 
 
-def combine_kernel(target_ref, *refs, count, terms):
-    pieces, sums, out = refs[:count], refs[count:-1], refs[-1]
-    slots = pieces[0].shape[0]
-    part_rows = out.shape[0] // PARTS
-    for k in range(PARTS):
-        target = target_ref[pl.ds(k * part_rows, part_rows), :]
-        delta = None
-        for d, piece in enumerate(pieces):
-            slot = d * slots + lax.broadcasted_iota(jnp.int32, (part_rows, slots), 1)
-            chosen = jnp.where(target == slot, 1.0, 0.0).astype(jnp.bfloat16)
-            term = dot_nn(chosen, piece[...])
-            delta = term if delta is None else delta + term
-        for x in sums[k * terms : (k + 1) * terms]:
-            delta = delta + x[...].astype(jnp.float32)
-        out[pl.ds(k * part_rows, part_rows), :] = delta.astype(jnp.bfloat16)
-
-
-def combine(target, pieces, sums):
-    terms = len(sums[0])
-    part_rows, width = sums[0][0].shape
+def combine_kernel(here_ref, row_ref, *refs, steps, resident, holders, count, starts):
+    pieces, sums, out = refs[:count], refs[count:-3], refs[-3]
+    chosen_ref, total_ref = refs[-2:]
+    slots, rolls = pieces[0].shape[0], row_ref.shape[1]
+    rows = out.shape[0]
+
+    @pl.when(pl.program_id(0) == 0)
+    def _():
+        _, place = row_slots(row_ref, here_ref[0], resident, holders)
+        shape = (rolls, count * slots)
+        slot = lax.broadcasted_iota(jnp.int32, shape, 1) // steps
+        picked = jnp.where(slot == jnp.broadcast_to(place, shape), 1.0, 0.0).astype(jnp.bfloat16)
+        shape = (rows, rolls)
+        roll = lax.broadcasted_iota(jnp.int32, shape, 0) // steps
+        spread = roll == lax.broadcasted_iota(jnp.int32, shape, 1)
+        chosen = dot_nn(jnp.where(spread, 1.0, 0.0).astype(jnp.bfloat16), picked)
+        shape = (rows, count * slots)
+        step = lax.broadcasted_iota(jnp.int32, shape, 0) % steps
+        aligned = step == lax.broadcasted_iota(jnp.int32, shape, 1) % steps
+        chosen_ref[...] = jnp.where(aligned, chosen, 0.0).astype(jnp.bfloat16)
+
+    stacked = jnp.concatenate([x[...] for x in pieces], axis=0)
+    total_ref[...] = dot_nn(chosen_ref[...], stacked)
+    for start, x in zip(starts, sums):
+        span = pl.ds(start, x.shape[0])
+        total_ref[span, :] += x[...].astype(jnp.float32)
+    out[...] = total_ref[...].astype(jnp.bfloat16)
+
+
+def combine(here, adapter_row, pieces, sums, steps, resident, holders):
+    width = pieces[0].shape[1]
     count = len(pieces)
-    flat = [x for part in sums for x in part]
-    rows = part_rows * len(sums)
+    starts, flat = zip(*sums)
+    rows = adapter_row.shape[1] * steps
+    block = min(width, 2 * HEAD_SIZE)
+
+    def columns(x):
+        return pl.BlockSpec((x, block), lambda j: (0, j))
+
     return pl.pallas_call(
-        functools.partial(combine_kernel, count=count, terms=terms),
+        functools.partial(
+            combine_kernel,
+            steps=steps,
+            resident=resident,
+            holders=holders,
+            count=count,
+            starts=starts,
+        ),
+        grid=(width // block,),
         out_shape=jax.ShapeDtypeStruct((rows, width), jnp.bfloat16),
-        in_specs=[VMEM] * (1 + count + len(flat)),
-        out_specs=VMEM,
-        compiler_params=pltpu.CompilerParams(vmem_limit_bytes=8 * MIB),
+        in_specs=[SMEM, pl.BlockSpec(adapter_row.shape, lambda j: (0, 0))]
+        + [columns(x.shape[0]) for x in (*pieces, *flat)],
+        out_specs=columns(rows),
+        scratch_shapes=[
+            pltpu.VMEM((rows, count * pieces[0].shape[0]), jnp.bfloat16),
+            pltpu.VMEM((rows, block), jnp.float32),
+        ],
+        compiler_params=pltpu.CompilerParams(vmem_limit_bytes=20 * MIB),
         cost_estimate=BRIEF,
-    )(target, *pieces, *flat)
+    )(here, adapter_row, *pieces, *flat)
 
 
 def local(
@@ -478,67 +584,65 @@
     own_expand = adapter_expand_weight.reshape(resident * rank, out_width)
     far = [(i, (i + block) % holders) for i in range(holders)]
 
-    adapter = rollout_adapter_index[:, 0]
-    holder = adapter // resident
-    order = jnp.arange(rolls, dtype=jnp.int32)
-    same = (adapter[:, None] == adapter[None, :]) & (order[None, :] < order[:, None])
-    turn = jnp.sum(same.astype(jnp.int32), axis=1)
-    fold = (here // block - holder // block) % FOLD
-    place = (holder % block - here % block) % block
-    slot = ((place * FOLD + fold) * resident + adapter % resident) * MOST + turn
-    target = (slot[:, None] * steps + jnp.arange(steps, dtype=jnp.int32)[None, :]).reshape(rows)
     slots = FOLD * resident * MOST * steps
     per_adapter = MOST * steps
-
-    code = (rollout_suffix_length * prefix_count + rollout_prefix_index % prefix_count)[None, :]
+    adapter_row = rollout_adapter_index.reshape(1, rolls)
+    lengths, prefixes = rollout_suffix_length[None, :], rollout_prefix_index[None, :]
     flat_queries = queries.reshape(rows, width)
     flat_fresh = fresh_key_value.reshape(2, rows, -1)
-    core_index = core.reshape(1).astype(jnp.int32)
+    here = here.reshape(1).astype(jnp.int32)
+    core = core.reshape(1).astype(jnp.int32)
     chip_index = chip.reshape(1).astype(jnp.int32)
-    cut = own_expand.shape[0] // CUTS
-    cuts = [own_expand[k * cut : (k + 1) * cut] for k in range(CUTS)]
+    blocks = rolls // BLOCK_ROLLS
+    early_blocks = blocks // 2
     tie = lax.optimization_barrier
 
-    def attend_part(code, part):
+    def attend_part(lengths, start, count):
         return attend(
-            code, flat_queries, shared_prefix_cache, rollout_suffix_cache, flat_fresh, steps, part
+            lengths, prefixes, flat_queries, shared_prefix_cache, rollout_suffix_cache,
+            flat_fresh, steps, start, count,
         )
 
-    def send_over_chips(pairs):
-        return [lax.ppermute(pairs[s], "tensor", over_chips(s)) for s in range(1, chips)]
-
-    code, target, cuts = tie((code, target, cuts))
+    def send_over_chips(away, cuts):
+        return [
+            lax.ppermute(x, "tensor", over_chips(1 + k // cuts)) for k, x in enumerate(away)
+        ]
+
+    def placed(start, own, came, cuts):
+        rows = own.shape[0] // cuts
+        return [(start, own)] + [(start + k % cuts * rows, x) for k, x in enumerate(came)]
+
     shrink = lax.ppermute(own_shrink, "adapter", far)
-    first = attend_part(code, 0)
-    send, keep = project(core_index, first, output_projection_weight, out_width)
+    first = attend_part(lengths, 0, early_blocks)
+    send, keep = project(core, first, output_projection_weight, out_width)
     come = lax.ppermute(send, "tensor", cores)
-    code, shrink, keep, cuts[0] = tie((code, shrink, keep, cuts[0]))
-    expands = [lax.ppermute(cuts[0], "adapter", far)]
-    second = attend_part(code, 1)
-    pairs = pair_sums(chip_index, keep, come)
-    second, expands[0], cuts[1], *pairs = tie((second, expands[0], cuts[1], *pairs))
-    expands.append(lax.ppermute(cuts[1], "adapter", far))
-    early = send_over_chips(pairs)
-    packed = list(pack(target[None, :], [first, second], block, slots))
-    second, packed[0] = tie((second, packed[0]))
+    lengths, shrink, keep, moved_expand = tie((lengths, shrink, keep, own_expand))
+    expand = lax.ppermute(moved_expand, "adapter", far)
+    second = attend_part(lengths, early_blocks, blocks - early_blocks)
+    own_early, *away = pair_sums(chip_index, keep, come, CUTS)
+    packed = list(
+        pack(here, adapter_row, [first, second], block, slots, steps, resident, holders)
+    )
+    second, packed[0], away = tie((second, packed[0], away))
+    early = send_over_chips(away, CUTS)
     pieces = [packed[0]] + [
         lax.ppermute(packed[d], "adapter", in_block(d)) for d in range(1, block)
     ]
-    send, keep = project(core_index, second, output_projection_weight, out_width)
-    late_pairs = pair_sums(chip_index, keep, lax.ppermute(send, "tensor", cores))
-    pieces[0], expands[1], early = tie((pieces[0], expands[1], early))
+    send, keep = project(core, second, output_projection_weight, out_width)
+    own_late, *away = pair_sums(chip_index, keep, lax.ppermute(send, "tensor", cores), 1)
+    pieces[0], expand, early = tie((pieces[0], expand, early))
     codes = shrink_rows([own_shrink, shrink], pieces, per_adapter, rank)
     codes = codes + lax.ppermute(codes, "tensor", cores)
     brief = codes.astype(jnp.bfloat16)
     codes = [brief] + [lax.ppermute(brief, "tensor", over_chips(s)) for s in range(1, chips)]
-    codes, late_pairs = tie((codes, late_pairs))
-    late = send_over_chips(late_pairs)
-    wide = expand_rows([own_expand, *expands], codes, per_adapter, rank, block)
+    codes, away = tie((codes, away))
+    late = send_over_chips(away, 1)
+    wide = expand_rows([own_expand, expand], codes, per_adapter, rank, block)
     back = [wide[0]] + [
         lax.ppermute(wide[d], "adapter", in_block(block - d)) for d in range(1, block)
     ]
-    sums = [[pairs[0], *early], [late_pairs[0], *late]]
-    mixed = combine(target[:, None], back, sums)
+    sums = placed(0, own_early, early, CUTS) + placed(first.shape[0], own_late, late, 1)
+    mixed = combine(here, adapter_row, back, sums, steps, resident, holders)
     return mixed.reshape(rolls, steps, out_width)
 
 

time: 112 us -> 102 us (0.911)
  local copies, waits for them, and re-layouts: 23.5 us -> 9.25 us
  Pallas kernels: 34.7 us -> 41.7 us
  other arithmetic: 2.38 us -> 0.02 us
  waiting for transfers between devices: 31.5 us -> 29.5 us
  starting transfers between devices: 18.8 us -> 20.7 us
    unnamed x32 -> x22, local copies, waits for them, and re-layouts: 17.7 us -> 4.74 us
    ppermute x4 -> x3, waiting for transfers between devices: 12.5 us -> 3.82 us  [the longest x2 2.46 us: send_over_chips(): lax.ppermute(x, 'tensor', over_chips(1 + k // cuts))]
    ppermute x3, waiting for transfers between devices: 0.01 us -> 6.91 us  [local(): lax.ppermute(packed[d], 'adapter', in_block(d))]
    pallas_call x2, Pallas kernels: 18.8 us -> 25.3 us  [attend(): pl.pallas_call(functools.partial(attend_kernel, steps=steps, group=group,...]
    ppermute x3, starting transfers between devices: 4.82 us -> 8.49 us  [local(): lax.ppermute(wide[d], 'adapter', in_block(block - d))]
    slice x1 -> x0, local copies, waits for them, and re-layouts: 1.79 us -> none  [local(): cuts = [own_expand[k * cut:(k + 1) * cut] for k in range(CUTS)]]
    ppermute x4 -> x3, starting transfers between devices: 4.25 us -> 2.56 us  [the longest x2 2.49 us: send_over_chips(): lax.ppermute(x, 'tensor', over_chips(1 + k // cuts))]
    ppermute x1, waiting for transfers between devices: 4.96 us -> 3.71 us  [local(): lax.ppermute(brief, 'tensor', over_chips(s))]
  transfers between devices with their start and end apart: 15 -> 14, of which waited for: 6 -> 8; matrix products, arithmetic and copies ran while one was open for 6% -> 3% of each run, Pallas kernels for 29% -> 38%
where the time goes in v2:
time: 102 us; the launch traced here: 101 us
  Pallas kernels  41.7 us (41%)
  waiting for transfers between devices  29.5 us (29%)
  starting transfers between devices  20.7 us (20%)
  local copies, waits for them, and re-layouts  9.25 us (9%)
    pallas_call x2, Pallas kernels, attend(): pl.pallas_call(functools.partial(attend_kernel, steps=steps, group=group,...  25.3 us
    ppermute x3, waiting for transfers between devices, local(): lax.ppermute(wide[d], 'adapter', in_block(block - d))  13.7 us
    ppermute x3, starting transfers between devices, local(): lax.ppermute(wide[d], 'adapter', in_block(block - d))  8.49 us
    pallas_call x2, Pallas kernels, project(): pl.pallas_call(functools.partial(project_kernel, count=count), grid_spec=...  8.23 us
    ppermute x3, waiting for transfers between devices, local(): lax.ppermute(packed[d], 'adapter', in_block(d))  6.91 us
    ppermute x3, starting transfers between devices, local(): lax.ppermute(packed[d], 'adapter', in_block(d))  4.89 us
    unnamed x22, local copies, waits for them, and re-layouts  4.74 us
    ppermute x1, starting transfers between devices, local(): shrink = lax.ppermute(own_shrink, 'adapter', far)  4.04 us
  transfers between devices with their start and end apart: 14, of which 8 were waited for; matrix products, arithmetic and copies ran while one was open for 3% of the time, Pallas kernels for 38%

profile of v2, /device:TPU:0, one launch (start us, length us, event | category | flops | bytes accessed | tf_op | source)
XLA Modules:
  0.0 101.3 jit_solution(13133904831051415306)
XLA Ops:
  0.0 4.0 %collective-permute-start = (bf16[256,1024]{1,0:T(8,128)(2,1)}, bf16[256,1024]{1,0:T(8,128)(2,1)}, u32[]{:S(2)}, u32[]{:S(2)}) collective-permute-start(bf16[256,1024]{1,0:T(8,128)(2,1)} %bitcast.12), channel_id=1, source_target_pairs={{0,16},{4,20},{8,24},{12,28},{16,0},{20,4},{24,8},{28,12},{1,17},{... | collective-permute-start | bytes 1572872 | tf_op jit(solution)/shard_map/ppermute | solution.py:615
  4.0 2.1 %reshape.32.q_ref = bf16[512,1024]{1,0:T(8,128)(2,1)} reshape(bf16[128,4,1024]{2,1,0:T(4,128)(2,1)} %param.10) | data formatting | bytes 2097152 | tf_op jit(solution)/shard_map/reshape | solution.py:591
  6.2 1.2 %reshape.33.fr_ref = bf16[2,512,256]{2,1,0:T(8,128)(2,1)S(1)} reshape(bf16[2,128,4,256]{3,2,1,0:T(4,128)(2,1)} %param.13) | data formatting | bytes 1048576 | tf_op jit(solution)/shard_map/reshape | solution.py:592
  7.3 0.0 copy-start.1
  7.3 0.0 copy-start.5
  7.4 0.7 copy-done.5
  8.0 0.0 copy-start.7
  8.0 0.7 copy-done.7
  8.7 12.2 %shard_map.100.a_ref.refs_0_ = bf16[256,1024]{1,0:T(8,128)(2,1)S(1)} custom-call(s32[1,128]{1,0:T(1,128)S(1)} %bitcast.14, s32[1,128]{1,0:T(1,128)S(1)} %bitcast.16, bf16[512,1024]{1,0:T(8,128)(2,1)} %reshape.32.q_ref, bf16[2,2,2048,256]{3,2,1,0:T(8,128)(2,1)} %kv_hbm.3, bf16[2,128,32,256]{3,2,1,0:T(8,128)(2,1)} %suf_hbm.3, ...), custom_call_target="tpu_custom_call" | custom-call | flops 8589934592 | bytes 16777216 | tf_op jit(solution)/shard_map/pallas_call | solution.py:247
  20.9 0.0 copy-done.1
  20.9 0.0 copy-start
  20.9 3.4 %copy-done = bf16[1024,4096]{1,0:T(8,128)(2,1)S(1)} copy-done((bf16[1024,4096]{1,0:T(8,128)(2,1)S(1)}, bf16[1024,4096]{1,0:T(8,128)(2,1)}, u32[]{:S(2)}) %copy-start) | copy-done | bytes 8388632
  24.3 0.0 copy-start.2
  24.3 0.0 copy-start.6
  24.3 0.0 copy-start.8
  24.3 4.5 %shard_map.101 = (bf16[2,256,1024]{2,1,0:T(8,128)(2,1)}, bf16[2,256,1024]{2,1,0:T(8,128)(2,1)S(1)}) custom-call(s32[1]{0:T(128)} %bitcast.5.core_ref, bf16[256,1024]{1,0:T(8,128)(2,1)S(1)} %shard_map.100.a_ref.refs_0_, bf16[1024,4096]{1,0:T(8,128)(2,1)S(1)} %copy-done), custom_call_target="tpu_custom_call" | custom-call | flops 1024 | bytes 1024 | tf_op jit(solution)/shard_map/pallas_call | solution.py:286
  28.8 0.0 collective-permute-start.1
  28.8 0.0 collective-permute-done.refs_1_
  28.8 0.0 slice-start
  28.8 0.0 copy-start.3
  28.8 0.0 slice-start.1
  28.9 0.1 collective-permute-start.2
  28.9 0.0 copy-done.2
  29.0 0.0 copy-done.6
  29.0 0.0 copy-done.8
  29.0 13.1 %shard_map.102.refs_1_.a_ref = bf16[256,1024]{1,0:T(8,128)(2,1)S(1)} custom-call(s32[1,128]{1,0:T(1,128)S(1)} %bitcast.15, s32[1,128]{1,0:T(1,128)S(1)} %bitcast.17, bf16[512,1024]{1,0:T(8,128)(2,1)} %reshape.32.q_ref, bf16[2,2,2048,256]{3,2,1,0:T(8,128)(2,1)} %kv_hbm.3, bf16[2,128,32,256]{3,2,1,0:T(8,128)(2,1)} %suf_hbm.3, bf16[2,512,256]{2,1,0:T(8,128)(2,1)S(1)} %copy-done.2), custom_call_target="tpu_custom_call" | custom-call | flops 8589934592 | bytes 16777216 | tf_op jit(solution)/shard_map/pallas_call | solution.py:247
  42.1 0.0 copy-done.3
  42.1 1.5 %shard_map.103 = (bf16[160,1024]{1,0:T(8,128)(2,1)S(1)}, bf16[160,1024]{1,0:T(8,128)(2,1)S(1)}, bf16[160,1024]{1,0:T(8,128)(2,1)S(1)}, bf16[160,1024]{1,0:T(8,128)(2,1)S(1)}) custom-call(s32[1]{0:T(128)} %bitcast.here_ref, s32[1,128]{1,0:T(1,128)S(1)} %bitcast.10, bf16[256,1024]{1,0:T(8,128)(2,1)S(1)} %shard_map.100.a_ref.refs_0_, ...), custom_call_target="tpu_custom_call" | custom-call | flops 1024 | bytes 1024 | tf_op jit(solution)/shard_map/pallas_call | solution.py:391
  43.6 0.0 collective-permute-done.1.come_ref
  43.6 0.2 shard_map.104
  43.9 1.9 %collective-permute-start.3 = (bf16[256,1024]{1,0:T(8,128)(2,1)S(1)}, bf16[256,1024]{1,0:T(8,128)(2,1)S(1)}, u32[]{:S(2)}, u32[]{:S(2)}) collective-permute-start(bf16[256,1024]{1,0:T(8,128)(2,1)S(1)} %get-tuple-element.42), channel_id=1, source_target_pairs={{0,2},{1,3},{2,0},{3,1},{4,6},{5,7},{6,4},{7,5},{8,10},{9,11},{10,... | collective-permute-start | bytes 1572872 | tf_op jit(solution)/shard_map/ppermute | solution.py:608
  45.8 1.5 %collective-permute-start.4 = (bf16[160,1024]{1,0:T(8,128)(2,1)S(1)}, bf16[160,1024]{1,0:T(8,128)(2,1)S(1)}, u32[]{:S(2)}, u32[]{:S(2)}) collective-permute-start(bf16[160,1024]{1,0:T(8,128)(2,1)S(1)} %get-tuple-element.46), channel_id=1, source_target_pairs={{0,4},{4,8},{8,12},{12,0},{16,20},{20,24},{24,28},{28,16},{1,5},{5... | collective-permute-start | bytes 983048 | tf_op jit(solution)/shard_map/ppermute | solution.py:629
  47.3 2.0 %collective-permute-start.5 = (bf16[160,1024]{1,0:T(8,128)(2,1)S(1)}, bf16[160,1024]{1,0:T(8,128)(2,1)S(1)}, u32[]{:S(2)}, u32[]{:S(2)}) collective-permute-start(bf16[160,1024]{1,0:T(8,128)(2,1)S(1)} %get-tuple-element.47), channel_id=1, source_target_pairs={{0,8},{4,12},{8,0},{12,4},{16,24},{20,28},{24,16},{28,20},{1,9},{5... | collective-permute-start | bytes 983048 | tf_op jit(solution)/shard_map/ppermute | solution.py:629
  49.3 0.0 copy-start.4
  49.3 1.4 %collective-permute-start.6 = (bf16[160,1024]{1,0:T(8,128)(2,1)S(1)}, bf16[160,1024]{1,0:T(8,128)(2,1)S(1)}, u32[]{:S(2)}, u32[]{:S(2)}) collective-permute-start(bf16[160,1024]{1,0:T(8,128)(2,1)S(1)} %get-tuple-element.48), channel_id=1, source_target_pairs={{0,12},{4,0},{8,4},{12,8},{16,28},{20,16},{24,20},{28,24},{1,13},{... | collective-permute-start | bytes 983048 | tf_op jit(solution)/shard_map/ppermute | solution.py:629
  50.7 0.0 slice-done
  50.7 0.0 slice-done.1
  50.7 3.7 %shard_map.106 = (bf16[2,256,1024]{2,1,0:T(8,128)(2,1)S(1)}, bf16[2,256,1024]{2,1,0:T(8,128)(2,1)S(1)}) custom-call(s32[1]{0:T(128)} %bitcast.5.core_ref, bf16[256,1024]{1,0:T(8,128)(2,1)S(1)} %shard_map.102.refs_1_.a_ref, bf16[1024,4096]{1,0:T(8,128)(2,1)S(1)} %bitcast.9), custom_call_target="tpu_custom_call" | custom-call | flops 1024 | bytes 1024 | tf_op jit(solution)/shard_map/pallas_call | solution.py:286
  54.4 1.4 %collective-permute-done.2.refs_1_ = bf16[256,1024]{1,0:T(8,128)(2,1)} collective-permute-done((bf16[256,1024]{1,0:T(8,128)(2,1)}, bf16[256,1024]{1,0:T(8,128)(2,1)}, u32[]{:S(2)}, u32[]{:S(2)}) %collective-permute-start.2) | collective-permute-done | bytes 524320 | tf_op jit(solution)/shard_map/ppermute | solution.py:620
  55.8 0.0 collective-permute-start.9
  55.8 2.5 %collective-permute-done.3.refs_5_ = bf16[256,1024]{1,0:T(8,128)(2,1)S(1)} collective-permute-done((bf16[256,1024]{1,0:T(8,128)(2,1)S(1)}, bf16[256,1024]{1,0:T(8,128)(2,1)S(1)}, u32[]{:S(2)}, u32[]{:S(2)}) %collective-permute-start.3) | collective-permute-done | bytes 524320 | tf_op jit(solution)/shard_map/ppermute | solution.py:608
  58.3 5.4 %collective-permute-done.4.refs_3_ = bf16[160,1024]{1,0:T(8,128)(2,1)S(1)} collective-permute-done((bf16[160,1024]{1,0:T(8,128)(2,1)S(1)}, bf16[160,1024]{1,0:T(8,128)(2,1)S(1)}, u32[]{:S(2)}, u32[]{:S(2)}) %collective-permute-start.4) | collective-permute-done | bytes 327712 | tf_op jit(solution)/shard_map/ppermute | solution.py:629
  63.7 0.0 collective-permute-done.5.refs_4_
  63.7 1.5 %collective-permute-done.6.refs_5_ = bf16[160,1024]{1,0:T(8,128)(2,1)S(1)} collective-permute-done((bf16[160,1024]{1,0:T(8,128)(2,1)S(1)}, bf16[160,1024]{1,0:T(8,128)(2,1)S(1)}, u32[]{:S(2)}, u32[]{:S(2)}) %collective-permute-start.6) | collective-permute-done | bytes 327712 | tf_op jit(solution)/shard_map/ppermute | solution.py:629
  65.2 0.0 copy-done.4
  65.2 1.7 %shard_map.105 = f32[320,128]{1,0:T(8,128)S(1)} custom-call(bf16[256,1024]{1,0:T(8,128)(2,1)S(1)} %bitcast.13, bf16[256,1024]{1,0:T(8,128)(2,1)} %collective-permute-done.refs_1_, bf16[160,1024]{1,0:T(8,128)(2,1)S(1)} %get-tuple-element.45.refs_2_, bf16[160,1024]{1,0:T(8,128)(2,1)S(1)} %collective-permute-done.4.refs_3_, ...), custom_call_target="tpu_custom_call" | custom-call | flops 8589934592 | bytes 16777216 | tf_op jit(solution)/shard_map/pallas_call | solution.py:438
  66.8 0.1 collective-permute-start.7
  66.9 1.4 %collective-permute-done.7 = f32[320,128]{1,0:T(8,128)S(1)} collective-permute-done((f32[320,128]{1,0:T(8,128)S(1)}, f32[320,128]{1,0:T(8,128)S(1)}, u32[]{:S(2)}, u32[]{:S(2)}) %collective-permute-start.7) | collective-permute-done | bytes 163872 | tf_op jit(solution)/shard_map/ppermute | solution.py:635
  68.3 0.6 collective-permute-start.8
  68.9 0.0 collective-permute-done.9.come_ref
  68.9 0.2 shard_map.107
  69.2 3.7 %collective-permute-done.8.refs_3_ = bf16[320,128]{1,0:T(8,128)(2,1)S(1)} collective-permute-done((bf16[320,128]{1,0:T(8,128)(2,1)S(1)}, bf16[320,128]{1,0:T(8,128)(2,1)S(1)}, u32[]{:S(2)}, u32[]{:S(2)}) %collective-permute-start.8) | collective-permute-done | bytes 81952 | tf_op jit(solution)/shard_map/ppermute | solution.py:637
  72.9 0.5 collective-permute-start.13
  73.4 1.8 %shard_map.108 = (bf16[160,1024]{1,0:T(8,128)(2,1)S(1)}, bf16[160,1024]{1,0:T(8,128)(2,1)S(1)}, bf16[160,1024]{1,0:T(8,128)(2,1)S(1)}, bf16[160,1024]{1,0:T(8,128)(2,1)S(1)}) custom-call(bf16[256,1024]{1,0:T(8,128)(2,1)} %bitcast.2.refs_0_, bf16[256,1024]{1,0:T(8,128)(2,1)} %collective-permute-done.2.refs_1_, bf16[320,128]{1,0:T(8,128)(2,1)S(1)} %add_convert_fusion.refs_2_, ...), custom_call_target="tpu_custom_call" | custom-call | flops 1024 | bytes 1024 | tf_op jit(solution)/shard_map/pallas_call | solution.py:480
  75.2 6.0 %collective-permute-start.10 = (bf16[160,1024]{1,0:T(8,128)(2,1)S(1)}, bf16[160,1024]{1,0:T(8,128)(2,1)S(1)}, u32[]{:S(2)}, u32[]{:S(2)}) collective-permute-start(bf16[160,1024]{1,0:T(8,128)(2,1)S(1)} %get-tuple-element.56), channel_id=1, source_target_pairs={{0,12},{4,0},{8,4},{12,8},{16,28},{20,16},{24,20},{28,24},{1,13},{... | collective-permute-start | bytes 983048 | tf_op jit(solution)/shard_map/ppermute | solution.py:642
  81.2 2.5 %collective-permute-start.11 = (bf16[160,1024]{1,0:T(8,128)(2,1)S(1)}, bf16[160,1024]{1,0:T(8,128)(2,1)S(1)}, u32[]{:S(2)}, u32[]{:S(2)}) collective-permute-start(bf16[160,1024]{1,0:T(8,128)(2,1)S(1)} %get-tuple-element.57), channel_id=1, source_target_pairs={{0,8},{4,12},{8,0},{12,4},{16,24},{20,28},{24,16},{28,20},{1,9},{5... | collective-permute-start | bytes 983048 | tf_op jit(solution)/shard_map/ppermute | solution.py:642
  83.7 0.0 collective-permute-start.12
  83.7 6.2 %collective-permute-done.10.refs_1_ = bf16[160,1024]{1,0:T(8,128)(2,1)S(1)} collective-permute-done((bf16[160,1024]{1,0:T(8,128)(2,1)S(1)}, bf16[160,1024]{1,0:T(8,128)(2,1)S(1)}, u32[]{:S(2)}, u32[]{:S(2)}) %collective-permute-start.10) | collective-permute-done | bytes 327712 | tf_op jit(solution)/shard_map/ppermute | solution.py:642
  89.9 7.5 %collective-permute-done.11.refs_2_ = bf16[160,1024]{1,0:T(8,128)(2,1)S(1)} collective-permute-done((bf16[160,1024]{1,0:T(8,128)(2,1)S(1)}, bf16[160,1024]{1,0:T(8,128)(2,1)S(1)}, u32[]{:S(2)}, u32[]{:S(2)}) %collective-permute-start.11) | collective-permute-done | bytes 327712 | tf_op jit(solution)/shard_map/ppermute | solution.py:642
  97.4 0.0 collective-permute-done.12.refs_3_
  97.4 0.0 collective-permute-done.13.refs_7_
  97.4 2.7 %shard_map.109 = bf16[512,1024]{1,0:T(8,128)(2,1)S(1)} custom-call(s32[1]{0:T(128)} %bitcast.here_ref, s32[1,128]{1,0:T(1,128)S(1)} %bitcast.11, bf16[160,1024]{1,0:T(8,128)(2,1)S(1)} %get-tuple-element.55.refs_0_, bf16[160,1024]{1,0:T(8,128)(2,1)S(1)} %collective-permute-done.10.refs_1_, bf16[160,1024]{1,0:T(8,128)(2,1)S(1)} %collective-permute-done.11.refs_2_, ...), custom_call_target="tpu_custom_call" | custom-call | flops 1024 | bytes 1024 | tf_op jit(solution)/shard_map/pallas_call | solution.py:531
  100.1 1.2 %reshape.35 = bf16[128,4,1024]{2,1,0:T(4,128)(2,1)} reshape(bf16[512,1024]{1,0:T(8,128)(2,1)S(1)} %shard_map.109) | data formatting | bytes 2097152 | tf_op jit(solution)/shard_map/reshape | solution.py:646
  (2 shorter events, 0.0 us)
Async XLA Ops:
  0.0 28.8 %collective-permute-start = (bf16[256,1024]{1,0:T(8,128)(2,1)}, bf16[256,1024]{1,0:T(8,128)(2,1)}, u32[]{:S(2)}, u32[]{:S(2)}) collective-permute-start(bf16[256,1024]{1,0:T(8,128)(2,1)} %bitcast.12), channel_id=1, source_target_pairs={{0,16},{4,20},{8,24},{12,28},{16,0},{20,4},{24,8},{28,12},{1,17},{... | collective-permute-start | bytes 1572872 | tf_op jit(solution)/shard_map/ppermute | solution.py:615
  7.3 13.5 %copy-start.1 = (bf16[2,512,256]{2,1,0:T(8,128)(2,1)}, bf16[2,512,256]{2,1,0:T(8,128)(2,1)S(1)}, u32[]{:S(2)}) copy-start(bf16[2,512,256]{2,1,0:T(8,128)(2,1)S(1)} %reshape.33.fr_ref) | copy-start | bytes 1572868
  7.3 0.7 copy-start.5
  8.0 0.7 copy-start.7
  20.9 3.4 %copy-start = (bf16[1024,4096]{1,0:T(8,128)(2,1)S(1)}, bf16[1024,4096]{1,0:T(8,128)(2,1)}, u32[]{:S(2)}) copy-start(bf16[1024,4096]{1,0:T(8,128)(2,1)} %w_ref.3) | copy-start | bytes 25165828
  24.3 4.7 %copy-start.2 = (bf16[2,512,256]{2,1,0:T(8,128)(2,1)S(1)}, bf16[2,512,256]{2,1,0:T(8,128)(2,1)}, u32[]{:S(2)}) copy-start(bf16[2,512,256]{2,1,0:T(8,128)(2,1)} %copy-done.1) | copy-start | bytes 1572868
  24.3 4.7 %copy-start.6 = (s32[128]{0:T(128)S(1)}, s32[128]{0:T(128)}, u32[]{:S(2)}) copy-start(s32[128]{0:T(128)} %param.15) | copy-start | bytes 1540
  24.3 4.7 %copy-start.8 = (s32[128]{0:T(128)S(1)}, s32[128]{0:T(128)}, u32[]{:S(2)}) copy-start(s32[128]{0:T(128)} %param.14) | copy-start | bytes 1540
  28.8 14.8 %collective-permute-start.1 = (bf16[2,256,1024]{2,1,0:T(8,128)(2,1)}, bf16[2,256,1024]{2,1,0:T(8,128)(2,1)S(1)}, u32[]{:S(2)}, u32[]{:S(2)}) collective-permute-start(bf16[2,256,1024]{2,1,0:T(8,128)(2,1)} %get-tuple-element.38), channel_id=1, source_target_pairs={{0,1},{1,0},{2,3},{3,2},{4,5},{5,4},{6,7},{7,6},{8,9},{9,8},{10,11... | collective-permute-start | bytes 3145736 | tf_op jit(solution)/shard_map/ppermute | solution.py:618
  28.8 21.9 %slice-start = ((s8[8388608]{0:T(1024)(128)(4,1)}), s8[4194304]{0:T(1024)(128)(4,1)S(1)}, s32[]{:S(2)}) async-start(s8[8388608]{0:T(1024)(128)(4,1)} %bitcast.8), calls=%async_computation | async-start | bytes 8388608
  28.8 13.2 %copy-start.3 = (s32[128,1]{0,1:T(1,128)S(1)}, s32[128,1]{0,1:T(1,128)}, u32[]{:S(2)}) copy-start(s32[128,1]{0,1:T(1,128)} %param.16) | copy-start | bytes 1540
  28.8 21.9 %slice-start.1 = ((s8[8388608]{0:T(1024)(128)(4,1)}), s8[4194304]{0:T(1024)(128)(4,1)S(1)}, s32[]{:S(2)}) async-start(s8[8388608]{0:T(1024)(128)(4,1)} %bitcast.8), calls=%async_computation.1 | async-start | bytes 8388608
  28.9 26.9 %collective-permute-start.2 = (bf16[256,1024]{1,0:T(8,128)(2,1)}, bf16[256,1024]{1,0:T(8,128)(2,1)}, u32[]{:S(2)}, u32[]{:S(2)}) collective-permute-start(bf16[256,1024]{1,0:T(8,128)(2,1)} %bitcast.2.refs_0_), channel_id=1, source_target_pairs={{0,16},{4,20},{8,24},{12,28},{16,0},{20,4},{24,8},{28,12},{1,17},{... | collective-permute-start | bytes 1572872 | tf_op jit(solution)/shard_map/ppermute | solution.py:620
  43.9 14.4 %collective-permute-start.3 = (bf16[256,1024]{1,0:T(8,128)(2,1)S(1)}, bf16[256,1024]{1,0:T(8,128)(2,1)S(1)}, u32[]{:S(2)}, u32[]{:S(2)}) collective-permute-start(bf16[256,1024]{1,0:T(8,128)(2,1)S(1)} %get-tuple-element.42), channel_id=1, source_target_pairs={{0,2},{1,3},{2,0},{3,1},{4,6},{5,7},{6,4},{7,5},{8,10},{9,11},{10,... | collective-permute-start | bytes 1572872 | tf_op jit(solution)/shard_map/ppermute | solution.py:608
  45.8 17.9 %collective-permute-start.4 = (bf16[160,1024]{1,0:T(8,128)(2,1)S(1)}, bf16[160,1024]{1,0:T(8,128)(2,1)S(1)}, u32[]{:S(2)}, u32[]{:S(2)}) collective-permute-start(bf16[160,1024]{1,0:T(8,128)(2,1)S(1)} %get-tuple-element.46), channel_id=1, source_target_pairs={{0,4},{4,8},{8,12},{12,0},{16,20},{20,24},{24,28},{28,16},{1,5},{5... | collective-permute-start | bytes 983048 | tf_op jit(solution)/shard_map/ppermute | solution.py:629
  47.3 16.3 %collective-permute-start.5 = (bf16[160,1024]{1,0:T(8,128)(2,1)S(1)}, bf16[160,1024]{1,0:T(8,128)(2,1)S(1)}, u32[]{:S(2)}, u32[]{:S(2)}) collective-permute-start(bf16[160,1024]{1,0:T(8,128)(2,1)S(1)} %get-tuple-element.47), channel_id=1, source_target_pairs={{0,8},{4,12},{8,0},{12,4},{16,24},{20,28},{24,16},{28,20},{1,9},{5... | collective-permute-start | bytes 983048 | tf_op jit(solution)/shard_map/ppermute | solution.py:629
  49.3 15.8 %copy-start.4 = (bf16[4,64,1024]{2,1,0:T(8,128)(2,1)S(1)}, bf16[4,64,1024]{2,1,0:T(8,128)(2,1)}, u32[]{:S(2)}) copy-start(bf16[4,64,1024]{2,1,0:T(8,128)(2,1)} %param.18) | copy-start | bytes 1572868
  49.3 15.8 %collective-permute-start.6 = (bf16[160,1024]{1,0:T(8,128)(2,1)S(1)}, bf16[160,1024]{1,0:T(8,128)(2,1)S(1)}, u32[]{:S(2)}, u32[]{:S(2)}) collective-permute-start(bf16[160,1024]{1,0:T(8,128)(2,1)S(1)} %get-tuple-element.48), channel_id=1, source_target_pairs={{0,12},{4,0},{8,4},{12,8},{16,28},{20,16},{24,20},{28,24},{1,13},{... | collective-permute-start | bytes 983048 | tf_op jit(solution)/shard_map/ppermute | solution.py:629
  55.8 13.1 %collective-permute-start.9 = (bf16[2,256,1024]{2,1,0:T(8,128)(2,1)S(1)}, bf16[2,256,1024]{2,1,0:T(8,128)(2,1)S(1)}, u32[]{:S(2)}, u32[]{:S(2)}) collective-permute-start(bf16[2,256,1024]{2,1,0:T(8,128)(2,1)S(1)} %get-tuple-element.51), channel_id=1, source_target_pairs={{0,1},{1,0},{2,3},{3,2},{4,5},{5,4},{6,7},{7,6},{8,9},{9,8},{10,11... | collective-permute-start | bytes 3145736 | tf_op jit(solution)/shard_map/ppermute | solution.py:632
  66.8 1.5 %collective-permute-start.7 = (f32[320,128]{1,0:T(8,128)S(1)}, f32[320,128]{1,0:T(8,128)S(1)}, u32[]{:S(2)}, u32[]{:S(2)}) collective-permute-start(f32[320,128]{1,0:T(8,128)S(1)} %shard_map.105), channel_id=1, source_target_pairs={{0,1},{1,0},{2,3},{3,2},{4,5},{5,4},{6,7},{7,6},{8,9},{9,8},{10,11... | collective-permute-start | bytes 491528 | tf_op jit(solution)/shard_map/ppermute | solution.py:635
  68.3 4.6 %collective-permute-start.8 = (bf16[320,128]{1,0:T(8,128)(2,1)S(1)}, bf16[320,128]{1,0:T(8,128)(2,1)S(1)}, u32[]{:S(2)}, u32[]{:S(2)}) collective-permute-start(bf16[320,128]{1,0:T(8,128)(2,1)S(1)} %add_convert_fusion.refs_2_), channel_id=1, source_target_pairs={{0,2},{1,3},{2,0},{3,1},{4,6},{5,7},{6,4},{7,5},{8,10},{9,11},{10,... | collective-permute-start | bytes 245768 | tf_op jit(solution)/shard_map/ppermute | solution.py:637
  72.9 24.5 %collective-permute-start.13 = (bf16[256,1024]{1,0:T(8,128)(2,1)S(1)}, bf16[256,1024]{1,0:T(8,128)(2,1)S(1)}, u32[]{:S(2)}, u32[]{:S(2)}) collective-permute-start(bf16[256,1024]{1,0:T(8,128)(2,1)S(1)} %get-tuple-element.62), channel_id=1, source_target_pairs={{0,2},{1,3},{2,0},{3,1},{4,6},{5,7},{6,4},{7,5},{8,10},{9,11},{10,... | collective-permute-start | bytes 1572872 | tf_op jit(solution)/shard_map/ppermute | solution.py:608
  75.2 14.7 %collective-permute-start.10 = (bf16[160,1024]{1,0:T(8,128)(2,1)S(1)}, bf16[160,1024]{1,0:T(8,128)(2,1)S(1)}, u32[]{:S(2)}, u32[]{:S(2)}) collective-permute-start(bf16[160,1024]{1,0:T(8,128)(2,1)S(1)} %get-tuple-element.56), channel_id=1, source_target_pairs={{0,12},{4,0},{8,4},{12,8},{16,28},{20,16},{24,20},{28,24},{1,13},{... | collective-permute-start | bytes 983048 | tf_op jit(solution)/shard_map/ppermute | solution.py:642
  81.2 16.2 %collective-permute-start.11 = (bf16[160,1024]{1,0:T(8,128)(2,1)S(1)}, bf16[160,1024]{1,0:T(8,128)(2,1)S(1)}, u32[]{:S(2)}, u32[]{:S(2)}) collective-permute-start(bf16[160,1024]{1,0:T(8,128)(2,1)S(1)} %get-tuple-element.57), channel_id=1, source_target_pairs={{0,8},{4,12},{8,0},{12,4},{16,24},{20,28},{24,16},{28,20},{1,9},{5... | collective-permute-start | bytes 983048 | tf_op jit(solution)/shard_map/ppermute | solution.py:642
  83.7 13.7 %collective-permute-start.12 = (bf16[160,1024]{1,0:T(8,128)(2,1)S(1)}, bf16[160,1024]{1,0:T(8,128)(2,1)S(1)}, u32[]{:S(2)}, u32[]{:S(2)}) collective-permute-start(bf16[160,1024]{1,0:T(8,128)(2,1)S(1)} %get-tuple-element.58), channel_id=1, source_target_pairs={{0,4},{4,8},{8,12},{12,0},{16,20},{20,24},{24,28},{28,16},{1,5},{5... | collective-permute-start | bytes 983048 | tf_op jit(solution)/shard_map/ppermute | solution.py:642
